TPU v7x, 128 devices: a whole 4x4x4 slice. The times are simulated.
128 devices in a mesh: row: 16 (over y_hi, z, core), col: 8 (over y_lo, x).
Axes of the slice: x: 4, y: 4 (y_hi: 2, y_lo: 2; y = y_hi * 2 + y_lo), z: 4, core: 2. Of those that a mesh axis runs over, the one named last changes fastest.
Arguments:
- features: bfloat16 [65536, 128], P(('row', 'col')), may hold values from -12 to 12
- tile_values: bfloat16 [16, 8, 512, 128, 128], P('row', 'col'), as said below
- tile_rows: int32 [16, 8, 512], P('row', 'col'), may hold values from 0 to 63, as said below
- tile_cols: int32 [16, 8, 512], P('row', 'col'), may hold values from 0 to 31
- tile_count: int32 [16, 8], P('row', 'col'), may hold values from 64 to 512, as said below
- weight1: bfloat16 [128, 256], replicated, may hold values from -0.5 to 0.5
- bias1: float32 [256], replicated, may hold values from -1 to 1
- weight2: bfloat16 [256, 256], replicated
- bias2: float32 [256], replicated, may hold values from -3 to 3
Outputs:
- node_out: bfloat16 [65536, 256], P(('row', 'col'))
Inputs may be any that keep to these rules, and one draw needn't show every extreme that they name: The pairs (tile_rows, tile_cols) of one device are distinct. Slots 0 to tile_count - 1 of a device hold its nonempty tiles; later slots are padding. `tile_values`: entries are nonnegative.
All inputs are finite; a program needn't handle non-finite values.
Results may differ from a plain program's by a relative error of at most 0.0037.
Values may be sent and summed in bfloat16 or wider, within the bound.
No kernel may reach another device: no remote copies, remote signals or barrier semaphores. Data moves between devices by JAX's collectives and lax.ppermute only.
A program may use at most 192 MiB of HBM per device.

v0:
```python
import functools

import jax
import jax.numpy as jnp
from jax import lax
from jax.experimental import pallas as pl
from jax.experimental.pallas import tpu as pltpu
from jax.sharding import PartitionSpec as P

F32 = jnp.float32
BF16 = jnp.bfloat16
I32 = jnp.int32
TILE = 128
EXTRA = 16
UNROLL = 16
CHUNK = 32
OUT = 1 << 16
SPAN = 64
CORES = 2
FAR_FIRST = (6, 5, 7, 2, 4, 1, 3)


def dot(a, b, dims):
    return lax.dot_general(a, b, (dims, ((), ())), preferred_element_type=F32)


def order_by(key, source, slot, live, earlier, keys):
    length = 3 * 128
    slots = key.shape[0]
    half = keys // 2
    lane = lax.broadcasted_iota(I32, (1, 128), 1)
    hot = jnp.where((key == lane) & live, 1.0, 0.0)
    prefix = dot(earlier, hot.astype(BF16), ((1,), (0,)))
    rank = jnp.sum(hot * prefix, axis=1, keepdims=True)
    count = jnp.sum(hot, axis=0, keepdims=True)
    pairs = jnp.floor((count + 1.0) * 0.5)
    from_key = lax.broadcasted_iota(I32, (128, 128), 0)
    to_key = lax.broadcasted_iota(I32, (128, 128), 1)
    below = jnp.where((from_key < to_key) & ((from_key >= half) | (to_key < half)), 1.0, 0.0)
    start = dot(jnp.broadcast_to(pairs, (8, 128)).astype(BF16), below.astype(BF16), ((1,), (0,)))[0:1]
    first_half = lax.broadcasted_iota(I32, (1, 128), 1) < half
    pairs0 = jnp.sum(jnp.where(first_half, pairs, 0.0), axis=1, keepdims=True)
    pairs1 = jnp.sum(jnp.where(first_half, 0.0, pairs), axis=1, keepdims=True)
    steps0 = jnp.floor((pairs0 + (UNROLL - 1.0)) * (1.0 / UNROLL))
    steps1 = steps0 + jnp.floor((pairs1 + (UNROLL - 1.0)) * (1.0 / UNROLL))
    start = start + jnp.where(first_half, 0.0, steps0 * UNROLL)
    place = 2.0 * jnp.sum(hot * start, axis=1, keepdims=True) + rank
    place = jnp.where(live, place, -1.0).astype(I32)
    empty = slots * SPAN
    code = slot * SPAN + source - empty
    position = 2 * lax.broadcasted_iota(I32, (1, length), 1)
    codes0 = jnp.sum(jnp.where(place == position, code, 0), axis=0, keepdims=True) + empty
    codes1 = jnp.sum(jnp.where(place == position + 1, code, 0), axis=0, keepdims=True) + empty
    start_col = jnp.transpose(jnp.broadcast_to(start, (8, 128)))[:, 0:1]
    key_id = lax.broadcasted_iota(I32, (128, 1), 0)
    pair_id = lax.broadcasted_iota(I32, (1, length), 1).astype(F32)
    reached = jnp.where(key_id < keys, start_col, 2.0**20) <= pair_id
    out_key = jnp.sum(jnp.where(reached, 1, 0), axis=0, keepdims=True) - 1
    out_block = jnp.where(out_key >= half, out_key - half, out_key)
    codes0 = codes0 + OUT * out_block
    rows = [codes[:, i : i + 128] for codes in (codes0, codes1) for i in range(0, length, 128)]
    rows.append(jnp.where(lane == 0, steps0, steps1).astype(I32))
    return jnp.concatenate(rows + [jnp.zeros((1, 128), I32)], axis=0)


def order_kernel(
    per_dev,
    row_blocks,
    col_blocks,
    count_ref,
    rows_ref,
    cols_ref,
    weight_ref,
    bias_ref,
    values_ref,
    first_ref,
    second_ref,
    tiles,
    weight_out,
    bias_out,
    sems,
    rows,
    cols,
    weight,
    bias,
    small_sems,
):
    slots = rows_ref.shape[1]
    count = count_ref[0, 0]
    small = [
        pltpu.make_async_copy(src, dst, small_sems.at[i])
        for i, (src, dst) in enumerate(
            ((rows_ref, rows), (cols_ref, cols), (weight_ref, weight), (bias_ref, bias))
        )
    ]
    for copy in small:
        copy.start()
    copies = [
        pltpu.make_async_copy(
            values_ref.at[pl.ds(i * CHUNK, CHUNK)], tiles.at[pl.ds(i * CHUNK, CHUNK)], sems.at[i]
        )
        for i in range(slots // CHUNK)
    ]
    for i, copy in enumerate(copies):
        pl.when(i * CHUNK < count)(functools.partial(copy.start, priority=1))
    tiles[slots] = jnp.zeros(tiles.shape[1:], tiles.dtype)

    earlier = lax.broadcasted_iota(I32, (1, slots), 1) < lax.broadcasted_iota(I32, (slots, 1), 0)
    earlier = jnp.where(earlier, 1.0, 0.0).astype(BF16)
    for copy in small:
        copy.wait()
    weight_out[...] = jnp.transpose(weight[...])
    bias_out[...] = jnp.transpose(jnp.broadcast_to(bias[...], (TILE, bias.shape[1])))
    index = jnp.concatenate([rows[...], cols[...], jnp.zeros((6, slots), I32)], axis=0)
    turned = jnp.transpose(index.astype(F32)).astype(I32)
    row, col = turned[:, 0:1], turned[:, 1:2]
    slot = lax.broadcasted_iota(I32, (slots, 1), 0)
    live = slot < count
    core = lax.axis_index("row") % CORES
    owner = row // per_dev
    in_half = (owner // CORES) * per_dev + row % per_dev
    own = (owner % CORES) == core
    half_rows = row_blocks // CORES
    key = jnp.where(own, half_rows, 0) + in_half
    first_ref[...] = order_by(key, col, slot, live, earlier, row_blocks)
    key = jnp.where(own, 0, col_blocks) + col
    second_ref[...] = order_by(key, in_half, slot, live, earlier, 2 * col_blocks)
    for i, copy in enumerate(copies):
        pl.when(i * CHUNK < count)(copy.wait)


def run_pairs(list_ref, half, tiles, source, acc, tile_dims):
    ones = jnp.ones((EXTRA, 2 * TILE), BF16)

    def step(i, carry):
        row, lane = i // (128 // UNROLL), i % (128 // UNROLL) * UNROLL
        blocks, sums = [], []
        for u in range(UNROLL):
            word = list_ref[row, lane + u]
            code0, code1 = word & (OUT - 1), list_ref[3 + row, lane + u]
            left = jnp.concatenate([source[code0 & (SPAN - 1)], source[code1 & (SPAN - 1)]], axis=1)
            left = jnp.concatenate([left, ones], axis=0)
            right = jnp.concatenate([tiles[code0 // SPAN], tiles[code1 // SPAN]], axis=tile_dims)
            blocks.append(word // OUT)
            sums.append(dot(left, right, ((1,), (tile_dims,))))
        for block, total in zip(blocks, sums):
            acc[block] += total
        return carry

    begin = 0 if half == 0 else list_ref[6, 0]
    lax.fori_loop(begin, list_ref[6, half], step, 0)


def parted(degree):
    high = degree.astype(BF16).astype(F32)
    return [high, degree - high]


def write_partials(block_of, out, d, per_dest, width):
    tails = []
    for j in range(per_dest):
        block, degree = block_of(d, j)
        out[pl.ds(j * width, width), :] = block.astype(BF16)
        tails += parted(degree)
    tails.append(jnp.zeros((EXTRA - 2 * per_dest, TILE), F32))
    out[pl.ds(per_dest * width, EXTRA), :] = jnp.concatenate(tails, axis=0).astype(BF16)


def on_diagonal(per_dev, other, add):
    row, col = lax.axis_index("row"), lax.axis_index("col")
    core = row % CORES
    which = 1 - core if other else core

    @pl.when(row // CORES == col)
    def _():
        def one(i, carry):
            m, t = i // per_dev, i % per_dev
            in_half = (core * per_dev + m) * per_dev + t
            add(in_half, (m * CORES + which) * per_dev + t)
            return carry

        lax.fori_loop(0, per_dev * per_dev, one, 0)


def lay_out(me, per_dev, pieces, out):
    for m, piece in enumerate(pieces):
        out[pl.ds((me ^ m) * per_dev, per_dev)] = piece[...]


def first_kernel(per_dev, half, n_col, list_ref, *refs):
    if half == 0:
        pieces, (tiles, out_ref, source, acc) = refs[:n_col], refs[n_col:]
        for m, piece in enumerate(pieces):
            first = (lax.axis_index("col") ^ m) * per_dev
            for j in range(per_dev):
                source[first + j] = jnp.transpose(piece[pl.ds(j * TILE, TILE), :])
    else:
        source, tiles, acc = refs
    acc[...] = jnp.zeros_like(acc)

    def add(in_half, col_block):
        acc[in_half, pl.ds(0, TILE), :] = source[col_block].astype(F32)

    on_diagonal(per_dev, half == 0, add)
    run_pairs(list_ref, half, tiles, source, acc, 1)
    if half == 0:

        def block_of(d, j):
            block = acc[d * per_dev + j]
            return block[:TILE], block[TILE : TILE + 1]

        def one(d, carry):
            write_partials(block_of, out_ref.at[d], d, per_dev, TILE)
            return carry

        lax.fori_loop(0, out_ref.shape[0], one, 0)


def join_kernel(per_dev, acc, parts_ref, *outs):
    def block_of(d, j):
        block = acc[d * per_dev + j]
        tail = parts_ref[d, pl.ds(per_dev * TILE, EXTRA), :].astype(F32)
        degree = block[TILE : TILE + 1] + (tail[2 * j : 2 * j + 1] + tail[2 * j + 1 : 2 * j + 2])
        return block[:TILE] + parts_ref[d, pl.ds(j * TILE, TILE), :].astype(F32), degree

    chip = lax.axis_index("row") // CORES
    for m, out in enumerate(outs):
        write_partials(block_of, out, chip ^ m, per_dev, TILE)


def gather_kernel(per_dev, *refs):
    lay_out(lax.axis_index("row") // CORES, per_dev, refs[:-1], refs[-1])


def second_kernel(per_dev, half, list_ref, mean_ref, weight_ref, bias_ref, tiles, *refs):
    if half == 0:
        out_ref, hidden = refs
        acc = out_ref
    else:
        before, out_ref, hidden, acc = refs
    width = hidden.shape[1]
    bias = jnp.concatenate([bias_ref[...], bias_ref[...]], axis=1)

    for b in range(0, hidden.shape[0], 2):
        means = jnp.concatenate([mean_ref[b], mean_ref[b + 1]], axis=1)
        both = jnp.maximum(dot(weight_ref[...], means, ((1,), (0,))) + bias, 0.0).astype(BF16)
        hidden[b] = both[:, :TILE]
        hidden[b + 1] = both[:, TILE:]
    acc[...] = jnp.zeros_like(acc)

    def add(in_half, col_block):
        acc[col_block, pl.ds(0, width), :] = hidden[in_half].astype(F32)

    on_diagonal(per_dev, half == 1, add)
    run_pairs(list_ref, half, tiles, hidden, acc, 0)
    if half == 1:

        def block_of(d, j):
            block = acc[d * per_dev + j] + before[d * per_dev + j]
            return block[:width], block[width : width + 1]

        def one(d, carry):
            write_partials(block_of, out_ref.at[d], d, per_dev, width)
            return carry

        lax.fori_loop(0, out_ref.shape[0], one, 0)


def total_mean(parts, j, per_dest, width):
    block = parts[0][pl.ds(j * width, width), :].astype(F32)
    tail = parts[0][pl.ds(per_dest * width, EXTRA), :].astype(F32)
    for part in parts[1:]:
        block += part[pl.ds(j * width, width), :].astype(F32)
        tail += part[pl.ds(per_dest * width, EXTRA), :].astype(F32)
    degree = 1.0 + (tail[2 * j : 2 * j + 1] + tail[2 * j + 1 : 2 * j + 2])
    return (block / degree).astype(BF16)


def mean_kernel(per_dest, *refs):
    parts, out_ref = refs[:-1], refs[-1]
    for j in range(per_dest):
        out_ref[j] = total_mean(parts, j, per_dest, TILE)


def last_kernel(per_dest, width, weight_ref, bias_ref, parts_ref, out_ref):
    parts = [parts_ref.at[s] for s in range(parts_ref.shape[0])]
    for j in range(per_dest):
        mean = total_mean(parts, j, per_dest, width)
        result = dot(mean, weight_ref[...], ((0,), (0,))) + bias_ref[...]
        out_ref[pl.ds(j * TILE, TILE), :] = result.astype(BF16)


def call(kernel, out, specs, scratch=(), limit=8, us=1):
    vmem = pl.BlockSpec(memory_space=pltpu.VMEM)
    return pl.pallas_call(
        kernel,
        out_shape=out,
        in_specs=specs,
        out_specs=jax.tree.map(lambda _: vmem, out),
        scratch_shapes=scratch,
        cost_estimate=pl.CostEstimate(flops=us * 10**9, bytes_accessed=us * 3 * 10**6, transcendentals=0),
        compiler_params=pltpu.CompilerParams(vmem_limit_bytes=limit * 1024 * 1024),
    )


def local(features, tile_values, tile_rows, tile_cols, tile_count, weight1, bias1, weight2, bias2):
    n_row, n_col = lax.axis_size("row"), lax.axis_size("col")
    rows_dev, in_width = features.shape
    width = weight1.shape[1]
    values = tile_values[0, 0]
    slots = values.shape[0]
    per_dev = rows_dev // TILE
    row_blocks, col_blocks = per_dev * n_row, per_dev * n_col
    half_rows = row_blocks // CORES
    chips = n_row // CORES
    count = tile_count.astype(I32)
    vmem = pl.BlockSpec(memory_space=pltpu.VMEM)
    smem = pl.BlockSpec(memory_space=pltpu.SMEM)
    hbm = pl.BlockSpec(memory_space=pltpu.HBM)
    shape = jax.ShapeDtypeStruct
    swap = [(i, i ^ 1) for i in range(n_row)]
    part = lambda rows: shape((per_dev * rows + EXTRA, TILE), BF16)

    def across(axis, n, step, pieces):
        came = {0: pieces[0]}
        for m in FAR_FIRST:
            came[m] = lax.ppermute(pieces[m], axis, [(i, i ^ (m * step)) for i in range(n)])
        return [came[m] for m in range(len(pieces))]

    pieces = across("col", n_col, 1, [features] * n_col)

    first_list, second_list, tiles, weight, bias = call(
        functools.partial(order_kernel, per_dev, row_blocks, col_blocks),
        (
            shape((8, 128), I32),
            shape((8, 128), I32),
            pltpu.VMEM((slots + 1, TILE, TILE), BF16),
            shape((width, in_width), BF16),
            shape((width, TILE), F32),
        ),
        [smem] + [hbm] * 5,
        [
            pltpu.SemaphoreType.DMA((slots // CHUNK,)),
            pltpu.VMEM((1, slots), I32),
            pltpu.VMEM((1, slots), I32),
            pltpu.VMEM((in_width, width), BF16),
            pltpu.VMEM((1, width), F32),
            pltpu.SemaphoreType.DMA((4,)),
        ],
        8,
        8,
    )(
        count,
        *(
            pltpu.with_memory_space_constraint(x, pltpu.HBM)
            for x in (tile_rows[0], tile_cols[0], weight1, bias1.reshape(1, width), values)
        ),
    )
    tiles = pltpu.with_memory_space_constraint(tiles, pltpu.VMEM)

    acc = (half_rows, in_width + EXTRA, TILE)
    away, source = call(
        functools.partial(first_kernel, per_dev, 0, n_col),
        (
            shape((chips, per_dev * in_width + EXTRA, TILE), BF16),
            shape((col_blocks, in_width, TILE), BF16),
        ),
        [smem] + [vmem] * (n_col + 1),
        [pltpu.VMEM(acc, F32)],
        8,
        4,
    )(first_list, *pieces, tiles)
    came = lax.ppermute(away, "row", swap)
    kept = call(
        functools.partial(first_kernel, per_dev, 1, n_col), shape(acc, F32), [smem, vmem, vmem], (), 8, 4
    )(first_list, source, tiles)
    first = call(
        functools.partial(join_kernel, per_dev), [part(in_width)] * chips, [vmem, vmem]
    )(kept, came)
    first = across("row", n_row, CORES, first)
    mean = call(
        functools.partial(mean_kernel, per_dev), shape((per_dev, in_width, TILE), BF16), [vmem] * chips
    )(*first)
    means = across("row", n_row, CORES, [mean] * chips)
    own = call(
        functools.partial(gather_kernel, per_dev), shape((half_rows, in_width, TILE), BF16), [vmem] * chips
    )(*means)
    other = lax.ppermute(own, "row", swap)

    acc = (col_blocks, width + EXTRA, TILE)
    hidden = pltpu.VMEM((half_rows, width, TILE), BF16)
    before = call(
        functools.partial(second_kernel, per_dev, 0),
        shape(acc, F32),
        [smem, vmem, vmem, vmem, vmem],
        [hidden],
        8,
        6,
    )(second_list, own, weight, bias, tiles)
    second = call(
        functools.partial(second_kernel, per_dev, 1),
        shape((n_col, per_dev * width + EXTRA, TILE), BF16),
        [smem, vmem, vmem, vmem, vmem, vmem],
        [hidden, pltpu.VMEM(acc, F32)],
        12,
        6,
    )(second_list, other, weight, bias, tiles, before)
    second = lax.all_to_all(second, "col", 0, 0)
    return call(
        functools.partial(last_kernel, per_dev, width),
        shape((rows_dev, width), BF16),
        [vmem] * 3,
    )(weight2, bias2.reshape(1, width), second)


def solution(mesh):
    in_specs = (
        P(("row", "col"), None),
        P("row", "col", None, None, None),
        P("row", "col", None),
        P("row", "col", None),
        P("row", "col"),
        P(),
        P(),
        P(),
        P(),
    )
    out_specs = P(("row", "col"), None)
    return jax.shard_map(local, mesh=mesh, in_specs=in_specs, out_specs=out_specs, check_vma=False)
```

profile of v0, /device:TPU:1, one launch (start us, length us, event | category | flops | bytes accessed | tf_op | source)
XLA Modules:
  0.0 116.8 jit_solution(17779373853499555439)
XLA Ops:
  0.0 4.6 %collective-permute-start.5 = (bf16[512,128]{1,0:T(8,128)(2,1)}, bf16[512,128]{1,0:T(8,128)(2,1)S(1)}, u32[]{:S(2)}, u32[]{:S(2)}) collective-permute-start(bf16[512,128]{1,0:T(8,128)(2,1)} %refs_0_.1), channel_id=1, source_target_pairs={{0,6},{1,7},{2,4},{3,5},{4,2},{5,3},{6,0},{7,1},{8,14},{9,15},{10,... | collective-permute-start | bytes 393224 | tf_op jit(solution)/shard_map/ppermute | solution.py:327
  4.6 0.2 collective-permute-start.4
  4.8 1.3 %collective-permute-start.3 = (bf16[512,128]{1,0:T(8,128)(2,1)}, bf16[512,128]{1,0:T(8,128)(2,1)S(1)}, u32[]{:S(2)}, u32[]{:S(2)}) collective-permute-start(bf16[512,128]{1,0:T(8,128)(2,1)} %refs_0_.1), channel_id=1, source_target_pairs={{0,4},{1,5},{2,6},{3,7},{4,0},{5,1},{6,2},{7,3},{8,12},{9,13},{10,... | collective-permute-start | bytes 393224 | tf_op jit(solution)/shard_map/ppermute | solution.py:327
  6.1 0.2 collective-permute-start.2
  6.3 2.7 %collective-permute-start.1 = (bf16[512,128]{1,0:T(8,128)(2,1)}, bf16[512,128]{1,0:T(8,128)(2,1)S(1)}, u32[]{:S(2)}, u32[]{:S(2)}) collective-permute-start(bf16[512,128]{1,0:T(8,128)(2,1)} %refs_0_.1), channel_id=1, source_target_pairs={{0,2},{1,3},{2,0},{3,1},{4,6},{5,7},{6,4},{7,5},{8,10},{9,11},{10,... | collective-permute-start | bytes 393224 | tf_op jit(solution)/shard_map/ppermute | solution.py:327
  9.7 0.4 collective-permute-start
  10.1 0.9 collective-permute-done.4.refs_5_
  11.0 2.0 %collective-permute-start.6 = (bf16[512,128]{1,0:T(8,128)(2,1)}, bf16[512,128]{1,0:T(8,128)(2,1)S(1)}, u32[]{:S(2)}, u32[]{:S(2)}) collective-permute-start(bf16[512,128]{1,0:T(8,128)(2,1)} %refs_0_.1), channel_id=1, source_target_pairs={{0,7},{1,6},{2,5},{3,4},{4,3},{5,2},{6,1},{7,0},{8,15},{9,14},{10,... | collective-permute-start | bytes 393224 | tf_op jit(solution)/shard_map/ppermute | solution.py:327
  13.0 4.1 %shard_map.91 = (s32[8,128]{1,0:T(8,128)S(1)}, s32[8,128]{1,0:T(8,128)S(1)}, bf16[513,128,128]{2,1,0:T(8,128)(2,1)S(1)}, bf16[256,128]{1,0:T(8,128)(2,1)S(1)}, f32[256,128]{1,0:T(8,128)S(1)}) custom-call(s32[1,1]{1,0:T(1,128)S(6)} %copy.10.count_ref, s32[1,512]{1,0:T(1,128)} %bitcast.7, s32[1,512]{1,0:T(1,128)} %bitcast.8, bf16[128,256]{1,0:T(8,128)(2,1)} %weight_ref.2, ...), custom_call_target="tpu_custom_call" | custom-call | flops 8000000000 | bytes 24000000 | tf_op jit(solution)/shard_map/pallas_call | solution.py:332
  17.1 0.0 collective-permute-done.1.refs_2_
  17.1 0.0 collective-permute-done.refs_1_
  17.1 0.3 collective-permute-done.6.refs_7_
  17.4 2.6 %shard_map.92 = (bf16[8,528,128]{2,1,0:T(8,128)(2,1)S(1)}, bf16[32,128,128]{2,1,0:T(8,128)(2,1)S(1)}) custom-call(s32[8,128]{1,0:T(8,128)S(1)} %get-tuple-element.21.list_ref, bf16[512,128]{1,0:T(8,128)(2,1)S(1)} %copy-done, bf16[512,128]{1,0:T(8,128)(2,1)S(1)} %collective-permute-done.refs_1_, bf16[512,128]{1,0:T(8,128)(2,1)S(1)} %collective-permute-done.1.refs_2_, ...), custom_call_target="tpu_custom_call" | custom-call | flops 4000000000 | bytes 12000000 | tf_op jit(solution)/shard_map/pallas_call | solution.py:362
  20.0 3.6 %collective-permute-start.7 = (bf16[8,528,128]{2,1,0:T(8,128)(2,1)S(1)}, bf16[8,528,128]{2,1,0:T(8,128)(2,1)S(1)}, u32[]{:S(2)}, u32[]{:S(2)}) collective-permute-start(bf16[8,528,128]{2,1,0:T(8,128)(2,1)S(1)} %get-tuple-element.24), channel_id=1, source_target_pairs={{0,8},{8,0},{16,24},{24,16},{32,40},{40,32},{48,56},{56,48},{64,72... | collective-permute-start | bytes 3244040 | tf_op jit(solution)/shard_map/ppermute | solution.py:373
  23.6 2.1 %shard_map.93.acc = f32[32,144,128]{2,1,0:T(8,128)S(1)} custom-call(s32[8,128]{1,0:T(8,128)S(1)} %get-tuple-element.21.list_ref, bf16[32,128,128]{2,1,0:T(8,128)(2,1)S(1)} %get-tuple-element.23.refs_0_, bf16[513,128,128]{2,1,0:T(8,128)(2,1)S(1)} %get-tuple-element.22.refs_8_.refs_1_.tiles), custom_call_target="tpu_custom_call" | custom-call | flops 4000000000 | bytes 12000000 | tf_op jit(solution)/shard_map/pallas_call | solution.py:374
  25.7 0.2 collective-permute-done.7.parts_ref
  25.9 0.3 shard_map.94
  26.2 3.8 %collective-permute-start.8 = (bf16[528,128]{1,0:T(8,128)(2,1)S(1)}, bf16[528,128]{1,0:T(8,128)(2,1)S(1)}, u32[]{:S(2)}, u32[]{:S(2)}) collective-permute-start(bf16[528,128]{1,0:T(8,128)(2,1)S(1)} %get-tuple-element.26), channel_id=1, source_target_pairs={{0,16},{8,24},{16,0},{24,8},{32,48},{40,56},{48,32},{56,40},{64,80... | collective-permute-start | bytes 405512 | tf_op jit(solution)/shard_map/ppermute | solution.py:327
  30.0 1.7 %collective-permute-start.9 = (bf16[528,128]{1,0:T(8,128)(2,1)S(1)}, bf16[528,128]{1,0:T(8,128)(2,1)S(1)}, u32[]{:S(2)}, u32[]{:S(2)}) collective-permute-start(bf16[528,128]{1,0:T(8,128)(2,1)S(1)} %get-tuple-element.27), channel_id=1, source_target_pairs={{0,32},{8,40},{16,48},{24,56},{32,0},{40,8},{48,16},{56,24},{64,96... | collective-permute-start | bytes 405512 | tf_op jit(solution)/shard_map/ppermute | solution.py:327
  31.6 0.8 collective-permute-start.10
  32.4 1.7 %collective-permute-start.11 = (bf16[528,128]{1,0:T(8,128)(2,1)S(1)}, bf16[528,128]{1,0:T(8,128)(2,1)S(1)}, u32[]{:S(2)}, u32[]{:S(2)}) collective-permute-start(bf16[528,128]{1,0:T(8,128)(2,1)S(1)} %get-tuple-element.29), channel_id=1, source_target_pairs={{0,64},{8,72},{16,80},{24,88},{32,96},{40,104},{48,112},{56,120},{... | collective-permute-start | bytes 405512 | tf_op jit(solution)/shard_map/ppermute | solution.py:327
  34.2 1.1 collective-permute-start.12
  35.3 5.0 %collective-permute-start.13 = (bf16[528,128]{1,0:T(8,128)(2,1)S(1)}, bf16[528,128]{1,0:T(8,128)(2,1)S(1)}, u32[]{:S(2)}, u32[]{:S(2)}) collective-permute-start(bf16[528,128]{1,0:T(8,128)(2,1)S(1)} %get-tuple-element.31), channel_id=1, source_target_pairs={{0,96},{8,104},{16,112},{24,120},{32,64},{40,72},{48,80},{56,88},{... | collective-permute-start | bytes 405512 | tf_op jit(solution)/shard_map/ppermute | solution.py:327
  40.3 0.0 collective-permute-done.9.refs_2_
  40.3 1.1 collective-permute-start.14
  41.4 3.6 %collective-permute-done.13.refs_6_ = bf16[528,128]{1,0:T(8,128)(2,1)S(1)} collective-permute-done((bf16[528,128]{1,0:T(8,128)(2,1)S(1)}, bf16[528,128]{1,0:T(8,128)(2,1)S(1)}, u32[]{:S(2)}, u32[]{:S(2)}) %collective-permute-start.13) | collective-permute-done | bytes 135200 | tf_op jit(solution)/shard_map/ppermute | solution.py:327
  45.0 3.7 %collective-permute-done.14.refs_7_ = bf16[528,128]{1,0:T(8,128)(2,1)S(1)} collective-permute-done((bf16[528,128]{1,0:T(8,128)(2,1)S(1)}, bf16[528,128]{1,0:T(8,128)(2,1)S(1)}, u32[]{:S(2)}, u32[]{:S(2)}) %collective-permute-start.14) | collective-permute-done | bytes 135200 | tf_op jit(solution)/shard_map/ppermute | solution.py:327
  48.8 0.2 shard_map.95.refs_0_
  48.9 1.9 %collective-permute-start.21 = (bf16[4,128,128]{2,1,0:T(8,128)(2,1)S(1)}, bf16[4,128,128]{2,1,0:T(8,128)(2,1)S(1)}, u32[]{:S(2)}, u32[]{:S(2)}) collective-permute-start(bf16[4,128,128]{2,1,0:T(8,128)(2,1)S(1)} %shard_map.95.refs_0_), channel_id=1, source_target_pairs={{0,112},{8,120},{16,96},{24,104},{32,80},{40,88},{48,64},{56,72},{... | collective-permute-start | bytes 393224 | tf_op jit(solution)/shard_map/ppermute | solution.py:327
  50.9 2.1 %collective-permute-start.20 = (bf16[4,128,128]{2,1,0:T(8,128)(2,1)S(1)}, bf16[4,128,128]{2,1,0:T(8,128)(2,1)S(1)}, u32[]{:S(2)}, u32[]{:S(2)}) collective-permute-start(bf16[4,128,128]{2,1,0:T(8,128)(2,1)S(1)} %shard_map.95.refs_0_), channel_id=1, source_target_pairs={{0,96},{8,104},{16,112},{24,120},{32,64},{40,72},{48,80},{56,88},{... | collective-permute-start | bytes 393224 | tf_op jit(solution)/shard_map/ppermute | solution.py:327
  52.9 3.0 %collective-permute-start.19 = (bf16[4,128,128]{2,1,0:T(8,128)(2,1)S(1)}, bf16[4,128,128]{2,1,0:T(8,128)(2,1)S(1)}, u32[]{:S(2)}, u32[]{:S(2)}) collective-permute-start(bf16[4,128,128]{2,1,0:T(8,128)(2,1)S(1)} %shard_map.95.refs_0_), channel_id=1, source_target_pairs={{0,80},{8,88},{16,64},{24,72},{32,112},{40,120},{48,96},{56,104},{... | collective-permute-start | bytes 393224 | tf_op jit(solution)/shard_map/ppermute | solution.py:327
  55.9 1.4 %collective-permute-start.18 = (bf16[4,128,128]{2,1,0:T(8,128)(2,1)S(1)}, bf16[4,128,128]{2,1,0:T(8,128)(2,1)S(1)}, u32[]{:S(2)}, u32[]{:S(2)}) collective-permute-start(bf16[4,128,128]{2,1,0:T(8,128)(2,1)S(1)} %shard_map.95.refs_0_), channel_id=1, source_target_pairs={{0,64},{8,72},{16,80},{24,88},{32,96},{40,104},{48,112},{56,120},{... | collective-permute-start | bytes 393224 | tf_op jit(solution)/shard_map/ppermute | solution.py:327
  57.3 0.7 collective-permute-start.17
  58.0 1.6 %collective-permute-start.16 = (bf16[4,128,128]{2,1,0:T(8,128)(2,1)S(1)}, bf16[4,128,128]{2,1,0:T(8,128)(2,1)S(1)}, u32[]{:S(2)}, u32[]{:S(2)}) collective-permute-start(bf16[4,128,128]{2,1,0:T(8,128)(2,1)S(1)} %shard_map.95.refs_0_), channel_id=1, source_target_pairs={{0,32},{8,40},{16,48},{24,56},{32,0},{40,8},{48,16},{56,24},{64,96... | collective-permute-start | bytes 393224 | tf_op jit(solution)/shard_map/ppermute | solution.py:327
  59.6 0.1 collective-permute-done.20.refs_6_
  59.7 2.2 %collective-permute-start.15 = (bf16[4,128,128]{2,1,0:T(8,128)(2,1)S(1)}, bf16[4,128,128]{2,1,0:T(8,128)(2,1)S(1)}, u32[]{:S(2)}, u32[]{:S(2)}) collective-permute-start(bf16[4,128,128]{2,1,0:T(8,128)(2,1)S(1)} %shard_map.95.refs_0_), channel_id=1, source_target_pairs={{0,16},{8,24},{16,0},{24,8},{32,48},{40,56},{48,32},{56,40},{64,80... | collective-permute-start | bytes 393224 | tf_op jit(solution)/shard_map/ppermute | solution.py:327
  61.9 2.4 %collective-permute-done.18.refs_4_ = bf16[4,128,128]{2,1,0:T(8,128)(2,1)S(1)} collective-permute-done((bf16[4,128,128]{2,1,0:T(8,128)(2,1)S(1)}, bf16[4,128,128]{2,1,0:T(8,128)(2,1)S(1)}, u32[]{:S(2)}, u32[]{:S(2)}) %collective-permute-start.18) | collective-permute-done | bytes 131104 | tf_op jit(solution)/shard_map/ppermute | solution.py:327
  64.3 0.7 collective-permute-done.17.refs_3_
  64.9 0.3 collective-permute-done.16.refs_2_
  65.2 1.4 %collective-permute-done.15.refs_1_ = bf16[4,128,128]{2,1,0:T(8,128)(2,1)S(1)} collective-permute-done((bf16[4,128,128]{2,1,0:T(8,128)(2,1)S(1)}, bf16[4,128,128]{2,1,0:T(8,128)(2,1)S(1)}, u32[]{:S(2)}, u32[]{:S(2)}) %collective-permute-start.15) | collective-permute-done | bytes 131104 | tf_op jit(solution)/shard_map/ppermute | solution.py:327
  66.6 0.1 shard_map.96.mean_ref
  66.7 2.9 %collective-permute-start.22 = (bf16[32,128,128]{2,1,0:T(8,128)(2,1)S(1)}, bf16[32,128,128]{2,1,0:T(8,128)(2,1)S(1)}, u32[]{:S(2)}, u32[]{:S(2)}) collective-permute-start(bf16[32,128,128]{2,1,0:T(8,128)(2,1)S(1)} %shard_map.96.mean_ref), channel_id=1, source_target_pairs={{0,8},{8,0},{16,24},{24,16},{32,40},{40,32},{48,56},{56,48},{64,72... | collective-permute-start | bytes 3145736 | tf_op jit(solution)/shard_map/ppermute | solution.py:388
  69.6 3.6 %shard_map.97.refs_0_ = f32[32,272,128]{2,1,0:T(8,128)S(1)} custom-call(s32[8,128]{1,0:T(8,128)S(1)} %get-tuple-element.20.list_ref, bf16[32,128,128]{2,1,0:T(8,128)(2,1)S(1)} %shard_map.96.mean_ref, bf16[256,128]{1,0:T(8,128)(2,1)S(1)} %get-tuple-element.33.weight_ref, f32[256,128]{1,0:T(8,128)S(1)} %get-tuple-element.34.bias_ref, ...), custom_call_target="tpu_custom_call" | custom-call | flops 6000000000 | bytes 18000000 | tf_op jit(solution)/shard_map/pallas_call | solution.py:392
  73.3 5.0 %shard_map.98 = bf16[8,1040,128]{2,1,0:T(8,128)(2,1)S(1)} custom-call(s32[8,128]{1,0:T(8,128)S(1)} %get-tuple-element.20.list_ref, bf16[32,128,128]{2,1,0:T(8,128)(2,1)S(1)} %collective-permute-done.22.mean_ref, bf16[256,128]{1,0:T(8,128)(2,1)S(1)} %get-tuple-element.33.weight_ref, f32[256,128]{1,0:T(8,128)S(1)} %get-tuple-element.34.bias_ref, ...), custom_call_target="tpu_custom_call" | custom-call | flops 6000000000 | bytes 18000000 | tf_op jit(solution)/shard_map/pallas_call | solution.py:400
  78.3 0.0 copy-start.1
  78.4 0.0 copy-start.2
  78.4 37.2 %all_to_all.5.parts_ref = bf16[8,1040,128]{2,1,0:T(8,128)(2,1)S(1)} all-to-all(bf16[8,1040,128]{2,1,0:T(8,128)(2,1)S(1)} %shard_map.98), channel_id=1, replica_groups=mesh['row'=16,'col'=8] {'col'}, dimensions={0} | all-to-all | bytes 4259840 | tf_op jit(solution)/shard_map/all_to_all | solution.py:408
  115.5 1.2 %shard_map.99 = bf16[512,256]{1,0:T(8,128)(2,1)} custom-call(bf16[256,256]{1,0:T(8,128)(2,1)S(1)} %copy-done.1, f32[1,256]{1,0:T(1,128)S(1)} %bitcast.5, bf16[8,1040,128]{2,1,0:T(8,128)(2,1)S(1)} %all_to_all.5.parts_ref), custom_call_target="tpu_custom_call" | custom-call | flops 1000000000 | bytes 3000000 | tf_op jit(solution)/shard_map/pallas_call | solution.py:409
  (14 shorter events, 0.0 us)
Async XLA Ops:
  0.0 9.7 %collective-permute-start.5 = (bf16[512,128]{1,0:T(8,128)(2,1)}, bf16[512,128]{1,0:T(8,128)(2,1)S(1)}, u32[]{:S(2)}, u32[]{:S(2)}) collective-permute-start(bf16[512,128]{1,0:T(8,128)(2,1)} %refs_0_.1), channel_id=1, source_target_pairs={{0,6},{1,7},{2,4},{3,5},{4,2},{5,3},{6,0},{7,1},{8,14},{9,15},{10,... | collective-permute-start | bytes 393224 | tf_op jit(solution)/shard_map/ppermute | solution.py:327
  4.6 6.4 %collective-permute-start.4 = (bf16[512,128]{1,0:T(8,128)(2,1)}, bf16[512,128]{1,0:T(8,128)(2,1)S(1)}, u32[]{:S(2)}, u32[]{:S(2)}) collective-permute-start(bf16[512,128]{1,0:T(8,128)(2,1)} %refs_0_.1), channel_id=1, source_target_pairs={{0,5},{1,4},{2,7},{3,6},{4,1},{5,0},{6,3},{7,2},{8,13},{9,12},{10,... | collective-permute-start | bytes 393224 | tf_op jit(solution)/shard_map/ppermute | solution.py:327
  4.8 12.3 %collective-permute-start.3 = (bf16[512,128]{1,0:T(8,128)(2,1)}, bf16[512,128]{1,0:T(8,128)(2,1)S(1)}, u32[]{:S(2)}, u32[]{:S(2)}) collective-permute-start(bf16[512,128]{1,0:T(8,128)(2,1)} %refs_0_.1), channel_id=1, source_target_pairs={{0,4},{1,5},{2,6},{3,7},{4,0},{5,1},{6,2},{7,3},{8,12},{9,13},{10,... | collective-permute-start | bytes 393224 | tf_op jit(solution)/shard_map/ppermute | solution.py:327
  6.1 11.0 %collective-permute-start.2 = (bf16[512,128]{1,0:T(8,128)(2,1)}, bf16[512,128]{1,0:T(8,128)(2,1)S(1)}, u32[]{:S(2)}, u32[]{:S(2)}) collective-permute-start(bf16[512,128]{1,0:T(8,128)(2,1)} %refs_0_.1), channel_id=1, source_target_pairs={{0,3},{1,2},{2,1},{3,0},{4,7},{5,6},{6,5},{7,4},{8,11},{9,10},{10,... | collective-permute-start | bytes 393224 | tf_op jit(solution)/shard_map/ppermute | solution.py:327
  6.3 10.8 %collective-permute-start.1 = (bf16[512,128]{1,0:T(8,128)(2,1)}, bf16[512,128]{1,0:T(8,128)(2,1)S(1)}, u32[]{:S(2)}, u32[]{:S(2)}) collective-permute-start(bf16[512,128]{1,0:T(8,128)(2,1)} %refs_0_.1), channel_id=1, source_target_pairs={{0,2},{1,3},{2,0},{3,1},{4,6},{5,7},{6,4},{7,5},{8,10},{9,11},{10,... | collective-permute-start | bytes 393224 | tf_op jit(solution)/shard_map/ppermute | solution.py:327
  9.7 7.4 %collective-permute-start = (bf16[512,128]{1,0:T(8,128)(2,1)}, bf16[512,128]{1,0:T(8,128)(2,1)S(1)}, u32[]{:S(2)}, u32[]{:S(2)}) collective-permute-start(bf16[512,128]{1,0:T(8,128)(2,1)} %refs_0_.1), channel_id=1, source_target_pairs={{0,1},{1,0},{2,3},{3,2},{4,5},{5,4},{6,7},{7,6},{8,9},{9,8},{10,11... | collective-permute-start | bytes 393224 | tf_op jit(solution)/shard_map/ppermute | solution.py:327
  11.0 6.4 %collective-permute-start.6 = (bf16[512,128]{1,0:T(8,128)(2,1)}, bf16[512,128]{1,0:T(8,128)(2,1)S(1)}, u32[]{:S(2)}, u32[]{:S(2)}) collective-permute-start(bf16[512,128]{1,0:T(8,128)(2,1)} %refs_0_.1), channel_id=1, source_target_pairs={{0,7},{1,6},{2,5},{3,4},{4,3},{5,2},{6,1},{7,0},{8,15},{9,14},{10,... | collective-permute-start | bytes 393224 | tf_op jit(solution)/shard_map/ppermute | solution.py:327
  13.0 4.4 %copy-start = (bf16[512,128]{1,0:T(8,128)(2,1)S(1)}, bf16[512,128]{1,0:T(8,128)(2,1)}, u32[]{:S(2)}) copy-start(bf16[512,128]{1,0:T(8,128)(2,1)} %refs_0_.1) | copy-start | bytes 393220
  20.0 5.9 %collective-permute-start.7 = (bf16[8,528,128]{2,1,0:T(8,128)(2,1)S(1)}, bf16[8,528,128]{2,1,0:T(8,128)(2,1)S(1)}, u32[]{:S(2)}, u32[]{:S(2)}) collective-permute-start(bf16[8,528,128]{2,1,0:T(8,128)(2,1)S(1)} %get-tuple-element.24), channel_id=1, source_target_pairs={{0,8},{8,0},{16,24},{24,16},{32,40},{40,32},{48,56},{56,48},{64,72... | collective-permute-start | bytes 3244040 | tf_op jit(solution)/shard_map/ppermute | solution.py:373
  26.2 9.1 %collective-permute-start.8 = (bf16[528,128]{1,0:T(8,128)(2,1)S(1)}, bf16[528,128]{1,0:T(8,128)(2,1)S(1)}, u32[]{:S(2)}, u32[]{:S(2)}) collective-permute-start(bf16[528,128]{1,0:T(8,128)(2,1)S(1)} %get-tuple-element.26), channel_id=1, source_target_pairs={{0,16},{8,24},{16,0},{24,8},{32,48},{40,56},{48,32},{56,40},{64,80... | collective-permute-start | bytes 405512 | tf_op jit(solution)/shard_map/ppermute | solution.py:327
  30.0 10.4 %collective-permute-start.9 = (bf16[528,128]{1,0:T(8,128)(2,1)S(1)}, bf16[528,128]{1,0:T(8,128)(2,1)S(1)}, u32[]{:S(2)}, u32[]{:S(2)}) collective-permute-start(bf16[528,128]{1,0:T(8,128)(2,1)S(1)} %get-tuple-element.27), channel_id=1, source_target_pairs={{0,32},{8,40},{16,48},{24,56},{32,0},{40,8},{48,16},{56,24},{64,96... | collective-permute-start | bytes 405512 | tf_op jit(solution)/shard_map/ppermute | solution.py:327
  31.6 9.8 %collective-permute-start.10 = (bf16[528,128]{1,0:T(8,128)(2,1)S(1)}, bf16[528,128]{1,0:T(8,128)(2,1)S(1)}, u32[]{:S(2)}, u32[]{:S(2)}) collective-permute-start(bf16[528,128]{1,0:T(8,128)(2,1)S(1)} %get-tuple-element.28), channel_id=1, source_target_pairs={{0,48},{8,56},{16,32},{24,40},{32,16},{40,24},{48,0},{56,8},{64,11... | collective-permute-start | bytes 405512 | tf_op jit(solution)/shard_map/ppermute | solution.py:327
  32.4 9.0 %collective-permute-start.11 = (bf16[528,128]{1,0:T(8,128)(2,1)S(1)}, bf16[528,128]{1,0:T(8,128)(2,1)S(1)}, u32[]{:S(2)}, u32[]{:S(2)}) collective-permute-start(bf16[528,128]{1,0:T(8,128)(2,1)S(1)} %get-tuple-element.29), channel_id=1, source_target_pairs={{0,64},{8,72},{16,80},{24,88},{32,96},{40,104},{48,112},{56,120},{... | collective-permute-start | bytes 405512 | tf_op jit(solution)/shard_map/ppermute | solution.py:327
  34.2 7.3 %collective-permute-start.12 = (bf16[528,128]{1,0:T(8,128)(2,1)S(1)}, bf16[528,128]{1,0:T(8,128)(2,1)S(1)}, u32[]{:S(2)}, u32[]{:S(2)}) collective-permute-start(bf16[528,128]{1,0:T(8,128)(2,1)S(1)} %get-tuple-element.30), channel_id=1, source_target_pairs={{0,80},{8,88},{16,64},{24,72},{32,112},{40,120},{48,96},{56,104},{... | collective-permute-start | bytes 405512 | tf_op jit(solution)/shard_map/ppermute | solution.py:327
  35.3 9.7 %collective-permute-start.13 = (bf16[528,128]{1,0:T(8,128)(2,1)S(1)}, bf16[528,128]{1,0:T(8,128)(2,1)S(1)}, u32[]{:S(2)}, u32[]{:S(2)}) collective-permute-start(bf16[528,128]{1,0:T(8,128)(2,1)S(1)} %get-tuple-element.31), channel_id=1, source_target_pairs={{0,96},{8,104},{16,112},{24,120},{32,64},{40,72},{48,80},{56,88},{... | collective-permute-start | bytes 405512 | tf_op jit(solution)/shard_map/ppermute | solution.py:327
  40.3 8.4 %collective-permute-start.14 = (bf16[528,128]{1,0:T(8,128)(2,1)S(1)}, bf16[528,128]{1,0:T(8,128)(2,1)S(1)}, u32[]{:S(2)}, u32[]{:S(2)}) collective-permute-start(bf16[528,128]{1,0:T(8,128)(2,1)S(1)} %get-tuple-element.32), channel_id=1, source_target_pairs={{0,112},{8,120},{16,96},{24,104},{32,80},{40,88},{48,64},{56,72},{... | collective-permute-start | bytes 405512 | tf_op jit(solution)/shard_map/ppermute | solution.py:327
  48.9 9.1 %collective-permute-start.21 = (bf16[4,128,128]{2,1,0:T(8,128)(2,1)S(1)}, bf16[4,128,128]{2,1,0:T(8,128)(2,1)S(1)}, u32[]{:S(2)}, u32[]{:S(2)}) collective-permute-start(bf16[4,128,128]{2,1,0:T(8,128)(2,1)S(1)} %shard_map.95.refs_0_), channel_id=1, source_target_pairs={{0,112},{8,120},{16,96},{24,104},{32,80},{40,88},{48,64},{56,72},{... | collective-permute-start | bytes 393224 | tf_op jit(solution)/shard_map/ppermute | solution.py:327
  50.9 8.8 %collective-permute-start.20 = (bf16[4,128,128]{2,1,0:T(8,128)(2,1)S(1)}, bf16[4,128,128]{2,1,0:T(8,128)(2,1)S(1)}, u32[]{:S(2)}, u32[]{:S(2)}) collective-permute-start(bf16[4,128,128]{2,1,0:T(8,128)(2,1)S(1)} %shard_map.95.refs_0_), channel_id=1, source_target_pairs={{0,96},{8,104},{16,112},{24,120},{32,64},{40,72},{48,80},{56,88},{... | collective-permute-start | bytes 393224 | tf_op jit(solution)/shard_map/ppermute | solution.py:327
  52.9 8.9 %collective-permute-start.19 = (bf16[4,128,128]{2,1,0:T(8,128)(2,1)S(1)}, bf16[4,128,128]{2,1,0:T(8,128)(2,1)S(1)}, u32[]{:S(2)}, u32[]{:S(2)}) collective-permute-start(bf16[4,128,128]{2,1,0:T(8,128)(2,1)S(1)} %shard_map.95.refs_0_), channel_id=1, source_target_pairs={{0,80},{8,88},{16,64},{24,72},{32,112},{40,120},{48,96},{56,104},{... | collective-permute-start | bytes 393224 | tf_op jit(solution)/shard_map/ppermute | solution.py:327
  55.9 8.4 %collective-permute-start.18 = (bf16[4,128,128]{2,1,0:T(8,128)(2,1)S(1)}, bf16[4,128,128]{2,1,0:T(8,128)(2,1)S(1)}, u32[]{:S(2)}, u32[]{:S(2)}) collective-permute-start(bf16[4,128,128]{2,1,0:T(8,128)(2,1)S(1)} %shard_map.95.refs_0_), channel_id=1, source_target_pairs={{0,64},{8,72},{16,80},{24,88},{32,96},{40,104},{48,112},{56,120},{... | collective-permute-start | bytes 393224 | tf_op jit(solution)/shard_map/ppermute | solution.py:327
  57.3 7.6 %collective-permute-start.17 = (bf16[4,128,128]{2,1,0:T(8,128)(2,1)S(1)}, bf16[4,128,128]{2,1,0:T(8,128)(2,1)S(1)}, u32[]{:S(2)}, u32[]{:S(2)}) collective-permute-start(bf16[4,128,128]{2,1,0:T(8,128)(2,1)S(1)} %shard_map.95.refs_0_), channel_id=1, source_target_pairs={{0,48},{8,56},{16,32},{24,40},{32,16},{40,24},{48,0},{56,8},{64,11... | collective-permute-start | bytes 393224 | tf_op jit(solution)/shard_map/ppermute | solution.py:327
  58.0 7.2 %collective-permute-start.16 = (bf16[4,128,128]{2,1,0:T(8,128)(2,1)S(1)}, bf16[4,128,128]{2,1,0:T(8,128)(2,1)S(1)}, u32[]{:S(2)}, u32[]{:S(2)}) collective-permute-start(bf16[4,128,128]{2,1,0:T(8,128)(2,1)S(1)} %shard_map.95.refs_0_), channel_id=1, source_target_pairs={{0,32},{8,40},{16,48},{24,56},{32,0},{40,8},{48,16},{56,24},{64,96... | collective-permute-start | bytes 393224 | tf_op jit(solution)/shard_map/ppermute | solution.py:327
  59.7 6.9 %collective-permute-start.15 = (bf16[4,128,128]{2,1,0:T(8,128)(2,1)S(1)}, bf16[4,128,128]{2,1,0:T(8,128)(2,1)S(1)}, u32[]{:S(2)}, u32[]{:S(2)}) collective-permute-start(bf16[4,128,128]{2,1,0:T(8,128)(2,1)S(1)} %shard_map.95.refs_0_), channel_id=1, source_target_pairs={{0,16},{8,24},{16,0},{24,8},{32,48},{40,56},{48,32},{56,40},{64,80... | collective-permute-start | bytes 393224 | tf_op jit(solution)/shard_map/ppermute | solution.py:327
  66.7 6.6 %collective-permute-start.22 = (bf16[32,128,128]{2,1,0:T(8,128)(2,1)S(1)}, bf16[32,128,128]{2,1,0:T(8,128)(2,1)S(1)}, u32[]{:S(2)}, u32[]{:S(2)}) collective-permute-start(bf16[32,128,128]{2,1,0:T(8,128)(2,1)S(1)} %shard_map.96.mean_ref), channel_id=1, source_target_pairs={{0,8},{8,0},{16,24},{24,16},{32,40},{40,32},{48,56},{56,48},{64,72... | collective-permute-start | bytes 3145736 | tf_op jit(solution)/shard_map/ppermute | solution.py:388
  78.3 37.2 %copy-start.1 = (bf16[256,256]{1,0:T(8,128)(2,1)S(1)}, bf16[256,256]{1,0:T(8,128)(2,1)}, u32[]{:S(2)}) copy-start(bf16[256,256]{1,0:T(8,128)(2,1)} %weight_ref.3) | copy-start | bytes 393220
  78.4 37.2 %copy-start.2 = (f32[256]{0:T(256)S(1)}, f32[256]{0:T(256)}, u32[]{:S(2)}) copy-start(f32[256]{0:T(256)} %param.17) | copy-start | bytes 3076
where the time goes:
time: 118 us; the launch traced here: 117 us
  starting transfers between devices  45.9 us (39%)
  blocking collectives  37.2 us (32%)
  Pallas kernels  19.2 us (16%)
  waiting for transfers between devices  13.7 us (12%)
    ppermute x21, starting transfers between devices, across(): lax.ppermute(pieces[m], axis, [(i, i ^ m * step) for i in range(n)])  39.4 us
    all_to_all x1, blocking collectives, local(): second = lax.all_to_all(second, 'col', 0, 0)  37.2 us
    ppermute x21, waiting for transfers between devices, across(): lax.ppermute(pieces[m], axis, [(i, i ^ m * step) for i in range(n)])  13.4 us
    pallas_call x1, Pallas kernels, local(): call(functools.partial(second_kernel, per_dev, 1), shape((n_col, per_dev...  5.05 us
    pallas_call x1, Pallas kernels, local(): call(functools.partial(order_kernel, per_dev, row_blocks, col_blocks), (s...  4.08 us
    pallas_call x1, Pallas kernels, local(): call(functools.partial(second_kernel, per_dev, 0), shape(acc, F32), [smem...  3.63 us
    ppermute x1, starting transfers between devices, local(): came = lax.ppermute(away, 'row', swap)  3.58 us
    ppermute x1, starting transfers between devices, local(): other = lax.ppermute(own, 'row', swap)  2.93 us
  transfers between devices with their start and end apart: 23, of which 10 were waited for; matrix products, arithmetic and copies ran while one was open for 0% of the time, Pallas kernels for 8%

commit v1 on v0

--- a/solution.py
+++ b/solution.py
@@ -380,7 +380,7 @@
     first = across("row", n_row, CORES, first)
     mean = call(
         functools.partial(mean_kernel, per_dev), shape((per_dev, in_width, TILE), BF16), [vmem] * chips
-    )(*first)
+    )(*first[::-1])
     means = across("row", n_row, CORES, [mean] * chips)
     own = call(
         functools.partial(gather_kernel, per_dev), shape((half_rows, in_width, TILE), BF16), [vmem] * chips

time: 118 us -> 117 us (level)
  starting transfers between devices: 45.9 us -> 40.1 us
  blocking collectives: 37.2 us -> 32.6 us
  Pallas kernels: 19.2 us -> 23.7 us
  waiting for transfers between devices: 13.7 us -> 17.4 us
    all_to_all x1, blocking collectives: 37.2 us -> 32.6 us  [local(): second = lax.all_to_all(second, 'col', 0, 0)]
    ppermute x21, waiting for transfers between devices: 13.4 us -> 17.4 us  [across(): lax.ppermute(pieces[m], axis, [(i, i ^ m * step) for i in range(n)])]
    ppermute x21, starting transfers between devices: 39.4 us -> 36.6 us  [across(): lax.ppermute(pieces[m], axis, [(i, i ^ m * step) for i in range(n)])]
    ppermute x1, starting transfers between devices: 3.58 us -> 1.94 us  [local(): came = lax.ppermute(away, 'row', swap)]
    pallas_call x1, Pallas kernels: 3.63 us -> 5.21 us  [local(): call(functools.partial(second_kernel, per_dev, 0), shape(acc, F32), [smem...]
    ppermute x1, starting transfers between devices: 2.93 us -> 1.5 us  [local(): other = lax.ppermute(own, 'row', swap)]
  transfers between devices with their start and end apart: 23 -> 23, of which waited for: 10 -> 10; matrix products, arithmetic and copies ran while one was open for 0% -> 0% of each run, Pallas kernels for 8% -> 11%
where the time goes in v1:
time: 117 us; the launch traced here: 115 us
  starting transfers between devices  40.1 us (34%)
  blocking collectives  32.6 us (28%)
  Pallas kernels  23.7 us (20%)
  waiting for transfers between devices  17.4 us (15%)
    ppermute x21, starting transfers between devices, across(): lax.ppermute(pieces[m], axis, [(i, i ^ m * step) for i in range(n)])  36.6 us
    all_to_all x1, blocking collectives, local(): second = lax.all_to_all(second, 'col', 0, 0)  32.6 us
    ppermute x21, waiting for transfers between devices, across(): lax.ppermute(pieces[m], axis, [(i, i ^ m * step) for i in range(n)])  17.4 us
    pallas_call x1, Pallas kernels, local(): call(functools.partial(second_kernel, per_dev, 1), shape((n_col, per_dev...  5.84 us
    pallas_call x1, Pallas kernels, local(): call(functools.partial(second_kernel, per_dev, 0), shape(acc, F32), [smem...  5.21 us
    pallas_call x1, Pallas kernels, local(): call(functools.partial(order_kernel, per_dev, row_blocks, col_blocks), (s...  4.07 us
    pallas_call x1, Pallas kernels, local(): call(functools.partial(first_kernel, per_dev, 0, n_col), (shape((chips, p...  3.7 us
    pallas_call x1, Pallas kernels, local(): call(functools.partial(first_kernel, per_dev, 1, n_col), shape(acc, F32),...  3.18 us
  transfers between devices with their start and end apart: 23, of which 10 were waited for; matrix products, arithmetic and copies ran while one was open for 0% of the time, Pallas kernels for 11%

profile of v1, /device:TPU:1, one launch (start us, length us, event | category | flops | bytes accessed | tf_op | source)
XLA Modules:
  0.0 114.6 jit_solution(3803668559310721982)
XLA Ops:
  0.0 4.6 %collective-permute-start.5 = (bf16[512,128]{1,0:T(8,128)(2,1)}, bf16[512,128]{1,0:T(8,128)(2,1)S(1)}, u32[]{:S(2)}, u32[]{:S(2)}) collective-permute-start(bf16[512,128]{1,0:T(8,128)(2,1)} %refs_0_.1), channel_id=1, source_target_pairs={{0,6},{1,7},{2,4},{3,5},{4,2},{5,3},{6,0},{7,1},{8,14},{9,15},{10,... | collective-permute-start | bytes 393224 | tf_op jit(solution)/shard_map/ppermute | solution.py:327
  4.6 0.2 collective-permute-start.4
  4.8 1.3 %collective-permute-start.3 = (bf16[512,128]{1,0:T(8,128)(2,1)}, bf16[512,128]{1,0:T(8,128)(2,1)S(1)}, u32[]{:S(2)}, u32[]{:S(2)}) collective-permute-start(bf16[512,128]{1,0:T(8,128)(2,1)} %refs_0_.1), channel_id=1, source_target_pairs={{0,4},{1,5},{2,6},{3,7},{4,0},{5,1},{6,2},{7,3},{8,12},{9,13},{10,... | collective-permute-start | bytes 393224 | tf_op jit(solution)/shard_map/ppermute | solution.py:327
  6.1 0.2 collective-permute-start.2
  6.3 2.7 %collective-permute-start.1 = (bf16[512,128]{1,0:T(8,128)(2,1)}, bf16[512,128]{1,0:T(8,128)(2,1)S(1)}, u32[]{:S(2)}, u32[]{:S(2)}) collective-permute-start(bf16[512,128]{1,0:T(8,128)(2,1)} %refs_0_.1), channel_id=1, source_target_pairs={{0,2},{1,3},{2,0},{3,1},{4,6},{5,7},{6,4},{7,5},{8,10},{9,11},{10,... | collective-permute-start | bytes 393224 | tf_op jit(solution)/shard_map/ppermute | solution.py:327
  9.7 0.0 collective-permute-done.5.refs_6_
  9.7 0.4 collective-permute-start
  10.1 0.9 collective-permute-done.4.refs_5_
  11.0 2.0 %collective-permute-start.6 = (bf16[512,128]{1,0:T(8,128)(2,1)}, bf16[512,128]{1,0:T(8,128)(2,1)S(1)}, u32[]{:S(2)}, u32[]{:S(2)}) collective-permute-start(bf16[512,128]{1,0:T(8,128)(2,1)} %refs_0_.1), channel_id=1, source_target_pairs={{0,7},{1,6},{2,5},{3,4},{4,3},{5,2},{6,1},{7,0},{8,15},{9,14},{10,... | collective-permute-start | bytes 393224 | tf_op jit(solution)/shard_map/ppermute | solution.py:327
  13.0 4.1 %shard_map.91 = (s32[8,128]{1,0:T(8,128)S(1)}, s32[8,128]{1,0:T(8,128)S(1)}, bf16[513,128,128]{2,1,0:T(8,128)(2,1)S(1)}, bf16[256,128]{1,0:T(8,128)(2,1)S(1)}, f32[256,128]{1,0:T(8,128)S(1)}) custom-call(s32[1,1]{1,0:T(1,128)S(6)} %copy.10.count_ref, s32[1,512]{1,0:T(1,128)} %bitcast.7, s32[1,512]{1,0:T(1,128)} %bitcast.8, bf16[128,256]{1,0:T(8,128)(2,1)} %weight_ref.2, ...), custom_call_target="tpu_custom_call" | custom-call | flops 8000000000 | bytes 24000000 | tf_op jit(solution)/shard_map/pallas_call | solution.py:332
  17.1 0.0 collective-permute-done.3.refs_4_
  17.1 0.0 collective-permute-done.1.refs_2_
  17.1 0.3 collective-permute-done.6.refs_7_
  17.4 3.7 %shard_map.92 = (bf16[8,528,128]{2,1,0:T(8,128)(2,1)S(1)}, bf16[32,128,128]{2,1,0:T(8,128)(2,1)S(1)}) custom-call(s32[8,128]{1,0:T(8,128)S(1)} %get-tuple-element.21.list_ref, bf16[512,128]{1,0:T(8,128)(2,1)S(1)} %copy-done, bf16[512,128]{1,0:T(8,128)(2,1)S(1)} %collective-permute-done.refs_1_, bf16[512,128]{1,0:T(8,128)(2,1)S(1)} %collective-permute-done.1.refs_2_, ...), custom_call_target="tpu_custom_call" | custom-call | flops 4000000000 | bytes 12000000 | tf_op jit(solution)/shard_map/pallas_call | solution.py:362
  21.1 1.9 %collective-permute-start.7 = (bf16[8,528,128]{2,1,0:T(8,128)(2,1)S(1)}, bf16[8,528,128]{2,1,0:T(8,128)(2,1)S(1)}, u32[]{:S(2)}, u32[]{:S(2)}) collective-permute-start(bf16[8,528,128]{2,1,0:T(8,128)(2,1)S(1)} %get-tuple-element.24), channel_id=1, source_target_pairs={{0,8},{8,0},{16,24},{24,16},{32,40},{40,32},{48,56},{56,48},{64,72... | collective-permute-start | bytes 3244040 | tf_op jit(solution)/shard_map/ppermute | solution.py:373
  23.1 3.2 %shard_map.93.acc = f32[32,144,128]{2,1,0:T(8,128)S(1)} custom-call(s32[8,128]{1,0:T(8,128)S(1)} %get-tuple-element.21.list_ref, bf16[32,128,128]{2,1,0:T(8,128)(2,1)S(1)} %get-tuple-element.23.refs_0_, bf16[513,128,128]{2,1,0:T(8,128)(2,1)S(1)} %get-tuple-element.22.refs_8_.refs_1_.tiles), custom_call_target="tpu_custom_call" | custom-call | flops 4000000000 | bytes 12000000 | tf_op jit(solution)/shard_map/pallas_call | solution.py:374
  26.3 0.3 shard_map.94
  26.5 6.1 %collective-permute-start.8 = (bf16[528,128]{1,0:T(8,128)(2,1)S(1)}, bf16[528,128]{1,0:T(8,128)(2,1)S(1)}, u32[]{:S(2)}, u32[]{:S(2)}) collective-permute-start(bf16[528,128]{1,0:T(8,128)(2,1)S(1)} %get-tuple-element.25), channel_id=1, source_target_pairs={{0,112},{8,120},{16,96},{24,104},{32,80},{40,88},{48,64},{56,72},{... | collective-permute-start | bytes 405512 | tf_op jit(solution)/shard_map/ppermute | solution.py:327
  32.7 1.0 collective-permute-start.9
  33.7 2.0 %collective-permute-start.10 = (bf16[528,128]{1,0:T(8,128)(2,1)S(1)}, bf16[528,128]{1,0:T(8,128)(2,1)S(1)}, u32[]{:S(2)}, u32[]{:S(2)}) collective-permute-start(bf16[528,128]{1,0:T(8,128)(2,1)S(1)} %get-tuple-element.27), channel_id=1, source_target_pairs={{0,80},{8,88},{16,64},{24,72},{32,112},{40,120},{48,96},{56,104},{... | collective-permute-start | bytes 405512 | tf_op jit(solution)/shard_map/ppermute | solution.py:327
  35.6 0.4 collective-permute-start.11
  36.0 2.3 %collective-permute-start.12 = (bf16[528,128]{1,0:T(8,128)(2,1)S(1)}, bf16[528,128]{1,0:T(8,128)(2,1)S(1)}, u32[]{:S(2)}, u32[]{:S(2)}) collective-permute-start(bf16[528,128]{1,0:T(8,128)(2,1)S(1)} %get-tuple-element.29), channel_id=1, source_target_pairs={{0,48},{8,56},{16,32},{24,40},{32,16},{40,24},{48,0},{56,8},{64,11... | collective-permute-start | bytes 405512 | tf_op jit(solution)/shard_map/ppermute | solution.py:327
  38.4 1.3 %collective-permute-start.13 = (bf16[528,128]{1,0:T(8,128)(2,1)S(1)}, bf16[528,128]{1,0:T(8,128)(2,1)S(1)}, u32[]{:S(2)}, u32[]{:S(2)}) collective-permute-start(bf16[528,128]{1,0:T(8,128)(2,1)S(1)} %get-tuple-element.30), channel_id=1, source_target_pairs={{0,32},{8,40},{16,48},{24,56},{32,0},{40,8},{48,16},{56,24},{64,96... | collective-permute-start | bytes 405512 | tf_op jit(solution)/shard_map/ppermute | solution.py:327
  39.6 2.1 %collective-permute-done.9.refs_1_ = bf16[528,128]{1,0:T(8,128)(2,1)S(1)} collective-permute-done((bf16[528,128]{1,0:T(8,128)(2,1)S(1)}, bf16[528,128]{1,0:T(8,128)(2,1)S(1)}, u32[]{:S(2)}, u32[]{:S(2)}) %collective-permute-start.9) | collective-permute-done | bytes 135200 | tf_op jit(solution)/shard_map/ppermute | solution.py:327
  41.8 0.2 collective-permute-done.10.refs_2_
  41.9 3.0 %collective-permute-done.11.refs_3_ = bf16[528,128]{1,0:T(8,128)(2,1)S(1)} collective-permute-done((bf16[528,128]{1,0:T(8,128)(2,1)S(1)}, bf16[528,128]{1,0:T(8,128)(2,1)S(1)}, u32[]{:S(2)}, u32[]{:S(2)}) %collective-permute-start.11) | collective-permute-done | bytes 135200 | tf_op jit(solution)/shard_map/ppermute | solution.py:327
  44.9 2.8 %collective-permute-done.13.refs_5_ = bf16[528,128]{1,0:T(8,128)(2,1)S(1)} collective-permute-done((bf16[528,128]{1,0:T(8,128)(2,1)S(1)}, bf16[528,128]{1,0:T(8,128)(2,1)S(1)}, u32[]{:S(2)}, u32[]{:S(2)}) %collective-permute-start.13) | collective-permute-done | bytes 135200 | tf_op jit(solution)/shard_map/ppermute | solution.py:327
  47.7 0.2 shard_map.95.refs_0_
  47.9 4.2 %collective-permute-start.21 = (bf16[4,128,128]{2,1,0:T(8,128)(2,1)S(1)}, bf16[4,128,128]{2,1,0:T(8,128)(2,1)S(1)}, u32[]{:S(2)}, u32[]{:S(2)}) collective-permute-start(bf16[4,128,128]{2,1,0:T(8,128)(2,1)S(1)} %shard_map.95.refs_0_), channel_id=1, source_target_pairs={{0,112},{8,120},{16,96},{24,104},{32,80},{40,88},{48,64},{56,72},{... | collective-permute-start | bytes 393224 | tf_op jit(solution)/shard_map/ppermute | solution.py:327
  52.1 0.4 collective-permute-start.20
  52.5 4.0 %collective-permute-start.19 = (bf16[4,128,128]{2,1,0:T(8,128)(2,1)S(1)}, bf16[4,128,128]{2,1,0:T(8,128)(2,1)S(1)}, u32[]{:S(2)}, u32[]{:S(2)}) collective-permute-start(bf16[4,128,128]{2,1,0:T(8,128)(2,1)S(1)} %shard_map.95.refs_0_), channel_id=1, source_target_pairs={{0,80},{8,88},{16,64},{24,72},{32,112},{40,120},{48,96},{56,104},{... | collective-permute-start | bytes 393224 | tf_op jit(solution)/shard_map/ppermute | solution.py:327
  56.4 0.4 collective-permute-start.18
  56.8 2.7 %collective-permute-start.17 = (bf16[4,128,128]{2,1,0:T(8,128)(2,1)S(1)}, bf16[4,128,128]{2,1,0:T(8,128)(2,1)S(1)}, u32[]{:S(2)}, u32[]{:S(2)}) collective-permute-start(bf16[4,128,128]{2,1,0:T(8,128)(2,1)S(1)} %shard_map.95.refs_0_), channel_id=1, source_target_pairs={{0,48},{8,56},{16,32},{24,40},{32,16},{40,24},{48,0},{56,8},{64,11... | collective-permute-start | bytes 393224 | tf_op jit(solution)/shard_map/ppermute | solution.py:327
  59.5 0.3 collective-permute-start.16
  59.8 0.0 collective-permute-done.20.refs_6_
  59.8 0.3 collective-permute-start.15
  60.1 1.6 %collective-permute-done.19.refs_5_ = bf16[4,128,128]{2,1,0:T(8,128)(2,1)S(1)} collective-permute-done((bf16[4,128,128]{2,1,0:T(8,128)(2,1)S(1)}, bf16[4,128,128]{2,1,0:T(8,128)(2,1)S(1)}, u32[]{:S(2)}, u32[]{:S(2)}) %collective-permute-start.19) | collective-permute-done | bytes 131104 | tf_op jit(solution)/shard_map/ppermute | solution.py:327
  61.7 3.0 %collective-permute-done.18.refs_4_ = bf16[4,128,128]{2,1,0:T(8,128)(2,1)S(1)} collective-permute-done((bf16[4,128,128]{2,1,0:T(8,128)(2,1)S(1)}, bf16[4,128,128]{2,1,0:T(8,128)(2,1)S(1)}, u32[]{:S(2)}, u32[]{:S(2)}) %collective-permute-start.18) | collective-permute-done | bytes 131104 | tf_op jit(solution)/shard_map/ppermute | solution.py:327
  64.7 1.8 %collective-permute-done.16.refs_2_ = bf16[4,128,128]{2,1,0:T(8,128)(2,1)S(1)} collective-permute-done((bf16[4,128,128]{2,1,0:T(8,128)(2,1)S(1)}, bf16[4,128,128]{2,1,0:T(8,128)(2,1)S(1)}, u32[]{:S(2)}, u32[]{:S(2)}) %collective-permute-start.16) | collective-permute-done | bytes 131104 | tf_op jit(solution)/shard_map/ppermute | solution.py:327
  66.5 1.6 %collective-permute-done.15.refs_1_ = bf16[4,128,128]{2,1,0:T(8,128)(2,1)S(1)} collective-permute-done((bf16[4,128,128]{2,1,0:T(8,128)(2,1)S(1)}, bf16[4,128,128]{2,1,0:T(8,128)(2,1)S(1)}, u32[]{:S(2)}, u32[]{:S(2)}) %collective-permute-start.15) | collective-permute-done | bytes 131104 | tf_op jit(solution)/shard_map/ppermute | solution.py:327
  68.1 0.1 shard_map.96.mean_ref
  68.2 1.5 %collective-permute-start.22 = (bf16[32,128,128]{2,1,0:T(8,128)(2,1)S(1)}, bf16[32,128,128]{2,1,0:T(8,128)(2,1)S(1)}, u32[]{:S(2)}, u32[]{:S(2)}) collective-permute-start(bf16[32,128,128]{2,1,0:T(8,128)(2,1)S(1)} %shard_map.96.mean_ref), channel_id=1, source_target_pairs={{0,8},{8,0},{16,24},{24,16},{32,40},{40,32},{48,56},{56,48},{64,72... | collective-permute-start | bytes 3145736 | tf_op jit(solution)/shard_map/ppermute | solution.py:388
  69.7 5.2 %shard_map.97.refs_0_ = f32[32,272,128]{2,1,0:T(8,128)S(1)} custom-call(s32[8,128]{1,0:T(8,128)S(1)} %get-tuple-element.20.list_ref, bf16[32,128,128]{2,1,0:T(8,128)(2,1)S(1)} %shard_map.96.mean_ref, bf16[256,128]{1,0:T(8,128)(2,1)S(1)} %get-tuple-element.33.weight_ref, f32[256,128]{1,0:T(8,128)S(1)} %get-tuple-element.34.bias_ref, ...), custom_call_target="tpu_custom_call" | custom-call | flops 6000000000 | bytes 18000000 | tf_op jit(solution)/shard_map/pallas_call | solution.py:392
  74.9 5.8 %shard_map.98 = bf16[8,1040,128]{2,1,0:T(8,128)(2,1)S(1)} custom-call(s32[8,128]{1,0:T(8,128)S(1)} %get-tuple-element.20.list_ref, bf16[32,128,128]{2,1,0:T(8,128)(2,1)S(1)} %collective-permute-done.22.mean_ref, bf16[256,128]{1,0:T(8,128)(2,1)S(1)} %get-tuple-element.33.weight_ref, f32[256,128]{1,0:T(8,128)S(1)} %get-tuple-element.34.bias_ref, ...), custom_call_target="tpu_custom_call" | custom-call | flops 6000000000 | bytes 18000000 | tf_op jit(solution)/shard_map/pallas_call | solution.py:400
  80.8 0.0 copy-start.1
  80.8 0.0 copy-start.2
  80.8 32.6 %all_to_all.5.parts_ref = bf16[8,1040,128]{2,1,0:T(8,128)(2,1)S(1)} all-to-all(bf16[8,1040,128]{2,1,0:T(8,128)(2,1)S(1)} %shard_map.98), channel_id=1, replica_groups=mesh['row'=16,'col'=8] {'col'}, dimensions={0} | all-to-all | bytes 4259840 | tf_op jit(solution)/shard_map/all_to_all | solution.py:408
  113.4 1.2 %shard_map.99 = bf16[512,256]{1,0:T(8,128)(2,1)} custom-call(bf16[256,256]{1,0:T(8,128)(2,1)S(1)} %copy-done.1, f32[1,256]{1,0:T(1,128)S(1)} %bitcast.5, bf16[8,1040,128]{2,1,0:T(8,128)(2,1)S(1)} %all_to_all.5.parts_ref), custom_call_target="tpu_custom_call" | custom-call | flops 1000000000 | bytes 3000000 | tf_op jit(solution)/shard_map/pallas_call | solution.py:409
  (14 shorter events, 0.0 us)
Async XLA Ops:
  0.0 9.7 %collective-permute-start.5 = (bf16[512,128]{1,0:T(8,128)(2,1)}, bf16[512,128]{1,0:T(8,128)(2,1)S(1)}, u32[]{:S(2)}, u32[]{:S(2)}) collective-permute-start(bf16[512,128]{1,0:T(8,128)(2,1)} %refs_0_.1), channel_id=1, source_target_pairs={{0,6},{1,7},{2,4},{3,5},{4,2},{5,3},{6,0},{7,1},{8,14},{9,15},{10,... | collective-permute-start | bytes 393224 | tf_op jit(solution)/shard_map/ppermute | solution.py:327
  4.6 6.4 %collective-permute-start.4 = (bf16[512,128]{1,0:T(8,128)(2,1)}, bf16[512,128]{1,0:T(8,128)(2,1)S(1)}, u32[]{:S(2)}, u32[]{:S(2)}) collective-permute-start(bf16[512,128]{1,0:T(8,128)(2,1)} %refs_0_.1), channel_id=1, source_target_pairs={{0,5},{1,4},{2,7},{3,6},{4,1},{5,0},{6,3},{7,2},{8,13},{9,12},{10,... | collective-permute-start | bytes 393224 | tf_op jit(solution)/shard_map/ppermute | solution.py:327
  4.8 12.3 %collective-permute-start.3 = (bf16[512,128]{1,0:T(8,128)(2,1)}, bf16[512,128]{1,0:T(8,128)(2,1)S(1)}, u32[]{:S(2)}, u32[]{:S(2)}) collective-permute-start(bf16[512,128]{1,0:T(8,128)(2,1)} %refs_0_.1), channel_id=1, source_target_pairs={{0,4},{1,5},{2,6},{3,7},{4,0},{5,1},{6,2},{7,3},{8,12},{9,13},{10,... | collective-permute-start | bytes 393224 | tf_op jit(solution)/shard_map/ppermute | solution.py:327
  6.1 11.0 %collective-permute-start.2 = (bf16[512,128]{1,0:T(8,128)(2,1)}, bf16[512,128]{1,0:T(8,128)(2,1)S(1)}, u32[]{:S(2)}, u32[]{:S(2)}) collective-permute-start(bf16[512,128]{1,0:T(8,128)(2,1)} %refs_0_.1), channel_id=1, source_target_pairs={{0,3},{1,2},{2,1},{3,0},{4,7},{5,6},{6,5},{7,4},{8,11},{9,10},{10,... | collective-permute-start | bytes 393224 | tf_op jit(solution)/shard_map/ppermute | solution.py:327
  6.3 10.8 %collective-permute-start.1 = (bf16[512,128]{1,0:T(8,128)(2,1)}, bf16[512,128]{1,0:T(8,128)(2,1)S(1)}, u32[]{:S(2)}, u32[]{:S(2)}) collective-permute-start(bf16[512,128]{1,0:T(8,128)(2,1)} %refs_0_.1), channel_id=1, source_target_pairs={{0,2},{1,3},{2,0},{3,1},{4,6},{5,7},{6,4},{7,5},{8,10},{9,11},{10,... | collective-permute-start | bytes 393224 | tf_op jit(solution)/shard_map/ppermute | solution.py:327
  9.7 7.4 %collective-permute-start = (bf16[512,128]{1,0:T(8,128)(2,1)}, bf16[512,128]{1,0:T(8,128)(2,1)S(1)}, u32[]{:S(2)}, u32[]{:S(2)}) collective-permute-start(bf16[512,128]{1,0:T(8,128)(2,1)} %refs_0_.1), channel_id=1, source_target_pairs={{0,1},{1,0},{2,3},{3,2},{4,5},{5,4},{6,7},{7,6},{8,9},{9,8},{10,11... | collective-permute-start | bytes 393224 | tf_op jit(solution)/shard_map/ppermute | solution.py:327
  11.0 6.4 %collective-permute-start.6 = (bf16[512,128]{1,0:T(8,128)(2,1)}, bf16[512,128]{1,0:T(8,128)(2,1)S(1)}, u32[]{:S(2)}, u32[]{:S(2)}) collective-permute-start(bf16[512,128]{1,0:T(8,128)(2,1)} %refs_0_.1), channel_id=1, source_target_pairs={{0,7},{1,6},{2,5},{3,4},{4,3},{5,2},{6,1},{7,0},{8,15},{9,14},{10,... | collective-permute-start | bytes 393224 | tf_op jit(solution)/shard_map/ppermute | solution.py:327
  13.0 4.4 %copy-start = (bf16[512,128]{1,0:T(8,128)(2,1)S(1)}, bf16[512,128]{1,0:T(8,128)(2,1)}, u32[]{:S(2)}) copy-start(bf16[512,128]{1,0:T(8,128)(2,1)} %refs_0_.1) | copy-start | bytes 393220
  21.1 5.1 %collective-permute-start.7 = (bf16[8,528,128]{2,1,0:T(8,128)(2,1)S(1)}, bf16[8,528,128]{2,1,0:T(8,128)(2,1)S(1)}, u32[]{:S(2)}, u32[]{:S(2)}) collective-permute-start(bf16[8,528,128]{2,1,0:T(8,128)(2,1)S(1)} %get-tuple-element.24), channel_id=1, source_target_pairs={{0,8},{8,0},{16,24},{24,16},{32,40},{40,32},{48,56},{56,48},{64,72... | collective-permute-start | bytes 3244040 | tf_op jit(solution)/shard_map/ppermute | solution.py:373
  26.5 11.8 %collective-permute-start.8 = (bf16[528,128]{1,0:T(8,128)(2,1)S(1)}, bf16[528,128]{1,0:T(8,128)(2,1)S(1)}, u32[]{:S(2)}, u32[]{:S(2)}) collective-permute-start(bf16[528,128]{1,0:T(8,128)(2,1)S(1)} %get-tuple-element.25), channel_id=1, source_target_pairs={{0,112},{8,120},{16,96},{24,104},{32,80},{40,88},{48,64},{56,72},{... | collective-permute-start | bytes 405512 | tf_op jit(solution)/shard_map/ppermute | solution.py:327
  32.7 9.1 %collective-permute-start.9 = (bf16[528,128]{1,0:T(8,128)(2,1)S(1)}, bf16[528,128]{1,0:T(8,128)(2,1)S(1)}, u32[]{:S(2)}, u32[]{:S(2)}) collective-permute-start(bf16[528,128]{1,0:T(8,128)(2,1)S(1)} %get-tuple-element.26), channel_id=1, source_target_pairs={{0,96},{8,104},{16,112},{24,120},{32,64},{40,72},{48,80},{56,88},{... | collective-permute-start | bytes 405512 | tf_op jit(solution)/shard_map/ppermute | solution.py:327
  33.7 8.2 %collective-permute-start.10 = (bf16[528,128]{1,0:T(8,128)(2,1)S(1)}, bf16[528,128]{1,0:T(8,128)(2,1)S(1)}, u32[]{:S(2)}, u32[]{:S(2)}) collective-permute-start(bf16[528,128]{1,0:T(8,128)(2,1)S(1)} %get-tuple-element.27), channel_id=1, source_target_pairs={{0,80},{8,88},{16,64},{24,72},{32,112},{40,120},{48,96},{56,104},{... | collective-permute-start | bytes 405512 | tf_op jit(solution)/shard_map/ppermute | solution.py:327
  35.6 9.3 %collective-permute-start.11 = (bf16[528,128]{1,0:T(8,128)(2,1)S(1)}, bf16[528,128]{1,0:T(8,128)(2,1)S(1)}, u32[]{:S(2)}, u32[]{:S(2)}) collective-permute-start(bf16[528,128]{1,0:T(8,128)(2,1)S(1)} %get-tuple-element.28), channel_id=1, source_target_pairs={{0,64},{8,72},{16,80},{24,88},{32,96},{40,104},{48,112},{56,120},{... | collective-permute-start | bytes 405512 | tf_op jit(solution)/shard_map/ppermute | solution.py:327
  36.0 8.9 %collective-permute-start.12 = (bf16[528,128]{1,0:T(8,128)(2,1)S(1)}, bf16[528,128]{1,0:T(8,128)(2,1)S(1)}, u32[]{:S(2)}, u32[]{:S(2)}) collective-permute-start(bf16[528,128]{1,0:T(8,128)(2,1)S(1)} %get-tuple-element.29), channel_id=1, source_target_pairs={{0,48},{8,56},{16,32},{24,40},{32,16},{40,24},{48,0},{56,8},{64,11... | collective-permute-start | bytes 405512 | tf_op jit(solution)/shard_map/ppermute | solution.py:327
  38.4 9.4 %collective-permute-start.13 = (bf16[528,128]{1,0:T(8,128)(2,1)S(1)}, bf16[528,128]{1,0:T(8,128)(2,1)S(1)}, u32[]{:S(2)}, u32[]{:S(2)}) collective-permute-start(bf16[528,128]{1,0:T(8,128)(2,1)S(1)} %get-tuple-element.30), channel_id=1, source_target_pairs={{0,32},{8,40},{16,48},{24,56},{32,0},{40,8},{48,16},{56,24},{64,96... | collective-permute-start | bytes 405512 | tf_op jit(solution)/shard_map/ppermute | solution.py:327
  41.8 6.0 %collective-permute-start.14 = (bf16[528,128]{1,0:T(8,128)(2,1)S(1)}, bf16[528,128]{1,0:T(8,128)(2,1)S(1)}, u32[]{:S(2)}, u32[]{:S(2)}) collective-permute-start(bf16[528,128]{1,0:T(8,128)(2,1)S(1)} %get-tuple-element.31), channel_id=1, source_target_pairs={{0,16},{8,24},{16,0},{24,8},{32,48},{40,56},{48,32},{56,40},{64,80... | collective-permute-start | bytes 405512 | tf_op jit(solution)/shard_map/ppermute | solution.py:327
  47.9 11.6 %collective-permute-start.21 = (bf16[4,128,128]{2,1,0:T(8,128)(2,1)S(1)}, bf16[4,128,128]{2,1,0:T(8,128)(2,1)S(1)}, u32[]{:S(2)}, u32[]{:S(2)}) collective-permute-start(bf16[4,128,128]{2,1,0:T(8,128)(2,1)S(1)} %shard_map.95.refs_0_), channel_id=1, source_target_pairs={{0,112},{8,120},{16,96},{24,104},{32,80},{40,88},{48,64},{56,72},{... | collective-permute-start | bytes 393224 | tf_op jit(solution)/shard_map/ppermute | solution.py:327
  52.1 7.7 %collective-permute-start.20 = (bf16[4,128,128]{2,1,0:T(8,128)(2,1)S(1)}, bf16[4,128,128]{2,1,0:T(8,128)(2,1)S(1)}, u32[]{:S(2)}, u32[]{:S(2)}) collective-permute-start(bf16[4,128,128]{2,1,0:T(8,128)(2,1)S(1)} %shard_map.95.refs_0_), channel_id=1, source_target_pairs={{0,96},{8,104},{16,112},{24,120},{32,64},{40,72},{48,80},{56,88},{... | collective-permute-start | bytes 393224 | tf_op jit(solution)/shard_map/ppermute | solution.py:327
  52.5 9.2 %collective-permute-start.19 = (bf16[4,128,128]{2,1,0:T(8,128)(2,1)S(1)}, bf16[4,128,128]{2,1,0:T(8,128)(2,1)S(1)}, u32[]{:S(2)}, u32[]{:S(2)}) collective-permute-start(bf16[4,128,128]{2,1,0:T(8,128)(2,1)S(1)} %shard_map.95.refs_0_), channel_id=1, source_target_pairs={{0,80},{8,88},{16,64},{24,72},{32,112},{40,120},{48,96},{56,104},{... | collective-permute-start | bytes 393224 | tf_op jit(solution)/shard_map/ppermute | solution.py:327
  56.4 8.3 %collective-permute-start.18 = (bf16[4,128,128]{2,1,0:T(8,128)(2,1)S(1)}, bf16[4,128,128]{2,1,0:T(8,128)(2,1)S(1)}, u32[]{:S(2)}, u32[]{:S(2)}) collective-permute-start(bf16[4,128,128]{2,1,0:T(8,128)(2,1)S(1)} %shard_map.95.refs_0_), channel_id=1, source_target_pairs={{0,64},{8,72},{16,80},{24,88},{32,96},{40,104},{48,112},{56,120},{... | collective-permute-start | bytes 393224 | tf_op jit(solution)/shard_map/ppermute | solution.py:327
  56.8 7.9 %collective-permute-start.17 = (bf16[4,128,128]{2,1,0:T(8,128)(2,1)S(1)}, bf16[4,128,128]{2,1,0:T(8,128)(2,1)S(1)}, u32[]{:S(2)}, u32[]{:S(2)}) collective-permute-start(bf16[4,128,128]{2,1,0:T(8,128)(2,1)S(1)} %shard_map.95.refs_0_), channel_id=1, source_target_pairs={{0,48},{8,56},{16,32},{24,40},{32,16},{40,24},{48,0},{56,8},{64,11... | collective-permute-start | bytes 393224 | tf_op jit(solution)/shard_map/ppermute | solution.py:327
  59.5 7.0 %collective-permute-start.16 = (bf16[4,128,128]{2,1,0:T(8,128)(2,1)S(1)}, bf16[4,128,128]{2,1,0:T(8,128)(2,1)S(1)}, u32[]{:S(2)}, u32[]{:S(2)}) collective-permute-start(bf16[4,128,128]{2,1,0:T(8,128)(2,1)S(1)} %shard_map.95.refs_0_), channel_id=1, source_target_pairs={{0,32},{8,40},{16,48},{24,56},{32,0},{40,8},{48,16},{56,24},{64,96... | collective-permute-start | bytes 393224 | tf_op jit(solution)/shard_map/ppermute | solution.py:327
  59.8 8.3 %collective-permute-start.15 = (bf16[4,128,128]{2,1,0:T(8,128)(2,1)S(1)}, bf16[4,128,128]{2,1,0:T(8,128)(2,1)S(1)}, u32[]{:S(2)}, u32[]{:S(2)}) collective-permute-start(bf16[4,128,128]{2,1,0:T(8,128)(2,1)S(1)} %shard_map.95.refs_0_), channel_id=1, source_target_pairs={{0,16},{8,24},{16,0},{24,8},{32,48},{40,56},{48,32},{56,40},{64,80... | collective-permute-start | bytes 393224 | tf_op jit(solution)/shard_map/ppermute | solution.py:327
  68.2 6.7 %collective-permute-start.22 = (bf16[32,128,128]{2,1,0:T(8,128)(2,1)S(1)}, bf16[32,128,128]{2,1,0:T(8,128)(2,1)S(1)}, u32[]{:S(2)}, u32[]{:S(2)}) collective-permute-start(bf16[32,128,128]{2,1,0:T(8,128)(2,1)S(1)} %shard_map.96.mean_ref), channel_id=1, source_target_pairs={{0,8},{8,0},{16,24},{24,16},{32,40},{40,32},{48,56},{56,48},{64,72... | collective-permute-start | bytes 3145736 | tf_op jit(solution)/shard_map/ppermute | solution.py:388
  80.8 32.6 %copy-start.1 = (bf16[256,256]{1,0:T(8,128)(2,1)S(1)}, bf16[256,256]{1,0:T(8,128)(2,1)}, u32[]{:S(2)}) copy-start(bf16[256,256]{1,0:T(8,128)(2,1)} %weight_ref.3) | copy-start | bytes 393220
  80.8 32.6 %copy-start.2 = (f32[256]{0:T(256)S(1)}, f32[256]{0:T(256)}, u32[]{:S(2)}) copy-start(f32[256]{0:T(256)} %param.17) | copy-start | bytes 3076

commit v2 on v1

--- a/solution.py
+++ b/solution.py
@@ -12,7 +12,7 @@
 I32 = jnp.int32
 TILE = 128
 EXTRA = 16
-UNROLL = 16
+UNROLL = 24
 CHUNK = 32
 OUT = 1 << 16
 SPAN = 64
@@ -41,8 +41,8 @@
     first_half = lax.broadcasted_iota(I32, (1, 128), 1) < half
     pairs0 = jnp.sum(jnp.where(first_half, pairs, 0.0), axis=1, keepdims=True)
     pairs1 = jnp.sum(jnp.where(first_half, 0.0, pairs), axis=1, keepdims=True)
-    steps0 = jnp.floor((pairs0 + (UNROLL - 1.0)) * (1.0 / UNROLL))
-    steps1 = steps0 + jnp.floor((pairs1 + (UNROLL - 1.0)) * (1.0 / UNROLL))
+    steps0 = jnp.floor((pairs0 + (UNROLL - 0.5)) * (1.0 / UNROLL))
+    steps1 = steps0 + jnp.floor((pairs1 + (UNROLL - 0.5)) * (1.0 / UNROLL))
     start = start + jnp.where(first_half, 0.0, steps0 * UNROLL)
     place = 2.0 * jnp.sum(hot * start, axis=1, keepdims=True) + rank
     place = jnp.where(live, place, -1.0).astype(I32)
@@ -133,11 +133,11 @@
     ones = jnp.ones((EXTRA, 2 * TILE), BF16)
 
     def step(i, carry):
-        row, lane = i // (128 // UNROLL), i % (128 // UNROLL) * UNROLL
         blocks, sums = [], []
         for u in range(UNROLL):
-            word = list_ref[row, lane + u]
-            code0, code1 = word & (OUT - 1), list_ref[3 + row, lane + u]
+            pair = i * UNROLL + u
+            word = list_ref[pair // 128, pair % 128]
+            code0, code1 = word & (OUT - 1), list_ref[3 + pair // 128, pair % 128]
             left = jnp.concatenate([source[code0 & (SPAN - 1)], source[code1 & (SPAN - 1)]], axis=1)
             left = jnp.concatenate([left, ones], axis=0)
             right = jnp.concatenate([tiles[code0 // SPAN], tiles[code1 // SPAN]], axis=tile_dims)

time: 117 us -> 117 us (level); the launches traced: 115 us -> 118 us
  blocking collectives: 32.6 us -> 37.5 us
  Pallas kernels: 23.7 us -> 20.4 us
  starting transfers between devices: 40.1 us -> 41.8 us
    all_to_all x1, blocking collectives: 32.6 us -> 37.5 us  [local(): second = lax.all_to_all(second, 'col', 0, 0)]
    pallas_call x1, Pallas kernels: 5.21 us -> 4.03 us  [local(): call(functools.partial(second_kernel, per_dev, 0), shape(acc, F32), [smem...]
  transfers between devices with their start and end apart: 23 -> 23, of which waited for: 10 -> 11; matrix products, arithmetic and copies ran while one was open for 0% -> 0% of each run, Pallas kernels for 11% -> 9%
where the time goes in v2:
time: 117 us; the launch traced here: 118 us
  starting transfers between devices  41.8 us (36%)
  blocking collectives  37.5 us (32%)
  Pallas kernels  20.4 us (17%)
  waiting for transfers between devices  17.3 us (15%)
    all_to_all x1, blocking collectives, local(): second = lax.all_to_all(second, 'col', 0, 0)  37.5 us
    ppermute x21, starting transfers between devices, across(): lax.ppermute(pieces[m], axis, [(i, i ^ m * step) for i in range(n)])  37 us
    ppermute x21, waiting for transfers between devices, across(): lax.ppermute(pieces[m], axis, [(i, i ^ m * step) for i in range(n)])  17.3 us
    pallas_call x1, Pallas kernels, local(): call(functools.partial(second_kernel, per_dev, 1), shape((n_col, per_dev...  4.82 us
    pallas_call x1, Pallas kernels, local(): call(functools.partial(order_kernel, per_dev, row_blocks, col_blocks), (s...  4.08 us
    pallas_call x1, Pallas kernels, local(): call(functools.partial(second_kernel, per_dev, 0), shape(acc, F32), [smem...  4.03 us
    pallas_call x1, Pallas kernels, local(): call(functools.partial(first_kernel, per_dev, 0, n_col), (shape((chips, p...  3.13 us
    ppermute x1, starting transfers between devices, local(): came = lax.ppermute(away, 'row', swap)  3.04 us
  transfers between devices with their start and end apart: 23, of which 11 were waited for; matrix products, arithmetic and copies ran while one was open for 0% of the time, Pallas kernels for 9%

profile of v2, /device:TPU:1, one launch (start us, length us, event | category | flops | bytes accessed | tf_op | source)
XLA Modules:
  0.0 117.9 jit_solution(168784142372285414)
XLA Ops:
  0.0 4.6 %collective-permute-start.5 = (bf16[512,128]{1,0:T(8,128)(2,1)}, bf16[512,128]{1,0:T(8,128)(2,1)S(1)}, u32[]{:S(2)}, u32[]{:S(2)}) collective-permute-start(bf16[512,128]{1,0:T(8,128)(2,1)} %refs_0_.1), channel_id=1, source_target_pairs={{0,6},{1,7},{2,4},{3,5},{4,2},{5,3},{6,0},{7,1},{8,14},{9,15},{10,... | collective-permute-start | bytes 393224 | tf_op jit(solution)/shard_map/ppermute | solution.py:327
  4.6 0.2 collective-permute-start.4
  4.8 1.3 %collective-permute-start.3 = (bf16[512,128]{1,0:T(8,128)(2,1)}, bf16[512,128]{1,0:T(8,128)(2,1)S(1)}, u32[]{:S(2)}, u32[]{:S(2)}) collective-permute-start(bf16[512,128]{1,0:T(8,128)(2,1)} %refs_0_.1), channel_id=1, source_target_pairs={{0,4},{1,5},{2,6},{3,7},{4,0},{5,1},{6,2},{7,3},{8,12},{9,13},{10,... | collective-permute-start | bytes 393224 | tf_op jit(solution)/shard_map/ppermute | solution.py:327
  6.1 0.2 collective-permute-start.2
  6.3 2.7 %collective-permute-start.1 = (bf16[512,128]{1,0:T(8,128)(2,1)}, bf16[512,128]{1,0:T(8,128)(2,1)S(1)}, u32[]{:S(2)}, u32[]{:S(2)}) collective-permute-start(bf16[512,128]{1,0:T(8,128)(2,1)} %refs_0_.1), channel_id=1, source_target_pairs={{0,2},{1,3},{2,0},{3,1},{4,6},{5,7},{6,4},{7,5},{8,10},{9,11},{10,... | collective-permute-start | bytes 393224 | tf_op jit(solution)/shard_map/ppermute | solution.py:327
  9.7 0.4 collective-permute-start
  10.1 0.9 collective-permute-done.4.refs_5_
  11.0 2.0 %collective-permute-start.6 = (bf16[512,128]{1,0:T(8,128)(2,1)}, bf16[512,128]{1,0:T(8,128)(2,1)S(1)}, u32[]{:S(2)}, u32[]{:S(2)}) collective-permute-start(bf16[512,128]{1,0:T(8,128)(2,1)} %refs_0_.1), channel_id=1, source_target_pairs={{0,7},{1,6},{2,5},{3,4},{4,3},{5,2},{6,1},{7,0},{8,15},{9,14},{10,... | collective-permute-start | bytes 393224 | tf_op jit(solution)/shard_map/ppermute | solution.py:327
  13.0 4.1 %shard_map.91 = (s32[8,128]{1,0:T(8,128)S(1)}, s32[8,128]{1,0:T(8,128)S(1)}, bf16[513,128,128]{2,1,0:T(8,128)(2,1)S(1)}, bf16[256,128]{1,0:T(8,128)(2,1)S(1)}, f32[256,128]{1,0:T(8,128)S(1)}) custom-call(s32[1,1]{1,0:T(1,128)S(6)} %copy.10.count_ref, s32[1,512]{1,0:T(1,128)} %bitcast.7, s32[1,512]{1,0:T(1,128)} %bitcast.8, bf16[128,256]{1,0:T(8,128)(2,1)} %weight_ref.2, ...), custom_call_target="tpu_custom_call" | custom-call | flops 8000000000 | bytes 24000000 | tf_op jit(solution)/shard_map/pallas_call | solution.py:332
  17.1 0.0 collective-permute-done.3.refs_4_
  17.1 0.0 collective-permute-done.1.refs_2_
  17.1 0.0 collective-permute-done.refs_1_
  17.1 0.3 collective-permute-done.6.refs_7_
  17.4 3.1 %shard_map.92 = (bf16[8,528,128]{2,1,0:T(8,128)(2,1)S(1)}, bf16[32,128,128]{2,1,0:T(8,128)(2,1)S(1)}) custom-call(s32[8,128]{1,0:T(8,128)S(1)} %get-tuple-element.21.list_ref, bf16[512,128]{1,0:T(8,128)(2,1)S(1)} %copy-done, bf16[512,128]{1,0:T(8,128)(2,1)S(1)} %collective-permute-done.refs_1_, bf16[512,128]{1,0:T(8,128)(2,1)S(1)} %collective-permute-done.1.refs_2_, ...), custom_call_target="tpu_custom_call" | custom-call | flops 4000000000 | bytes 12000000 | tf_op jit(solution)/shard_map/pallas_call | solution.py:362
  20.6 3.0 %collective-permute-start.7 = (bf16[8,528,128]{2,1,0:T(8,128)(2,1)S(1)}, bf16[8,528,128]{2,1,0:T(8,128)(2,1)S(1)}, u32[]{:S(2)}, u32[]{:S(2)}) collective-permute-start(bf16[8,528,128]{2,1,0:T(8,128)(2,1)S(1)} %get-tuple-element.24), channel_id=1, source_target_pairs={{0,8},{8,0},{16,24},{24,16},{32,40},{40,32},{48,56},{56,48},{64,72... | collective-permute-start | bytes 3244040 | tf_op jit(solution)/shard_map/ppermute | solution.py:373
  23.6 2.6 %shard_map.93.acc = f32[32,144,128]{2,1,0:T(8,128)S(1)} custom-call(s32[8,128]{1,0:T(8,128)S(1)} %get-tuple-element.21.list_ref, bf16[32,128,128]{2,1,0:T(8,128)(2,1)S(1)} %get-tuple-element.23.refs_0_, bf16[513,128,128]{2,1,0:T(8,128)(2,1)S(1)} %get-tuple-element.22.refs_8_.refs_1_.tiles), custom_call_target="tpu_custom_call" | custom-call | flops 4000000000 | bytes 12000000 | tf_op jit(solution)/shard_map/pallas_call | solution.py:374
  26.2 0.3 shard_map.94
  26.5 7.0 %collective-permute-start.8 = (bf16[528,128]{1,0:T(8,128)(2,1)S(1)}, bf16[528,128]{1,0:T(8,128)(2,1)S(1)}, u32[]{:S(2)}, u32[]{:S(2)}) collective-permute-start(bf16[528,128]{1,0:T(8,128)(2,1)S(1)} %get-tuple-element.25), channel_id=1, source_target_pairs={{0,112},{8,120},{16,96},{24,104},{32,80},{40,88},{48,64},{56,72},{... | collective-permute-start | bytes 405512 | tf_op jit(solution)/shard_map/ppermute | solution.py:327
  33.4 0.0 collective-permute-start.9
  33.4 1.1 collective-permute-start.10
  34.5 2.3 %collective-permute-start.11 = (bf16[528,128]{1,0:T(8,128)(2,1)S(1)}, bf16[528,128]{1,0:T(8,128)(2,1)S(1)}, u32[]{:S(2)}, u32[]{:S(2)}) collective-permute-start(bf16[528,128]{1,0:T(8,128)(2,1)S(1)} %get-tuple-element.28), channel_id=1, source_target_pairs={{0,64},{8,72},{16,80},{24,88},{32,96},{40,104},{48,112},{56,120},{... | collective-permute-start | bytes 405512 | tf_op jit(solution)/shard_map/ppermute | solution.py:327
  36.8 2.3 %collective-permute-start.12 = (bf16[528,128]{1,0:T(8,128)(2,1)S(1)}, bf16[528,128]{1,0:T(8,128)(2,1)S(1)}, u32[]{:S(2)}, u32[]{:S(2)}) collective-permute-start(bf16[528,128]{1,0:T(8,128)(2,1)S(1)} %get-tuple-element.29), channel_id=1, source_target_pairs={{0,48},{8,56},{16,32},{24,40},{32,16},{40,24},{48,0},{56,8},{64,11... | collective-permute-start | bytes 405512 | tf_op jit(solution)/shard_map/ppermute | solution.py:327
  39.1 0.6 collective-permute-start.13
  39.7 1.6 %collective-permute-done.9.refs_1_ = bf16[528,128]{1,0:T(8,128)(2,1)S(1)} collective-permute-done((bf16[528,128]{1,0:T(8,128)(2,1)S(1)}, bf16[528,128]{1,0:T(8,128)(2,1)S(1)}, u32[]{:S(2)}, u32[]{:S(2)}) %collective-permute-start.9) | collective-permute-done | bytes 135200 | tf_op jit(solution)/shard_map/ppermute | solution.py:327
  41.3 1.6 %collective-permute-done.10.refs_2_ = bf16[528,128]{1,0:T(8,128)(2,1)S(1)} collective-permute-done((bf16[528,128]{1,0:T(8,128)(2,1)S(1)}, bf16[528,128]{1,0:T(8,128)(2,1)S(1)}, u32[]{:S(2)}, u32[]{:S(2)}) %collective-permute-start.10) | collective-permute-done | bytes 135200 | tf_op jit(solution)/shard_map/ppermute | solution.py:327
  42.9 2.9 %collective-permute-done.11.refs_3_ = bf16[528,128]{1,0:T(8,128)(2,1)S(1)} collective-permute-done((bf16[528,128]{1,0:T(8,128)(2,1)S(1)}, bf16[528,128]{1,0:T(8,128)(2,1)S(1)}, u32[]{:S(2)}, u32[]{:S(2)}) %collective-permute-start.11) | collective-permute-done | bytes 135200 | tf_op jit(solution)/shard_map/ppermute | solution.py:327
  45.8 2.0 %collective-permute-done.13.refs_5_ = bf16[528,128]{1,0:T(8,128)(2,1)S(1)} collective-permute-done((bf16[528,128]{1,0:T(8,128)(2,1)S(1)}, bf16[528,128]{1,0:T(8,128)(2,1)S(1)}, u32[]{:S(2)}, u32[]{:S(2)}) %collective-permute-start.13) | collective-permute-done | bytes 135200 | tf_op jit(solution)/shard_map/ppermute | solution.py:327
  47.8 0.4 collective-permute-done.14.refs_6_
  48.2 0.2 shard_map.95.refs_0_
  48.4 2.3 %collective-permute-start.21 = (bf16[4,128,128]{2,1,0:T(8,128)(2,1)S(1)}, bf16[4,128,128]{2,1,0:T(8,128)(2,1)S(1)}, u32[]{:S(2)}, u32[]{:S(2)}) collective-permute-start(bf16[4,128,128]{2,1,0:T(8,128)(2,1)S(1)} %shard_map.95.refs_0_), channel_id=1, source_target_pairs={{0,112},{8,120},{16,96},{24,104},{32,80},{40,88},{48,64},{56,72},{... | collective-permute-start | bytes 393224 | tf_op jit(solution)/shard_map/ppermute | solution.py:327
  50.7 4.2 %collective-permute-start.20 = (bf16[4,128,128]{2,1,0:T(8,128)(2,1)S(1)}, bf16[4,128,128]{2,1,0:T(8,128)(2,1)S(1)}, u32[]{:S(2)}, u32[]{:S(2)}) collective-permute-start(bf16[4,128,128]{2,1,0:T(8,128)(2,1)S(1)} %shard_map.95.refs_0_), channel_id=1, source_target_pairs={{0,96},{8,104},{16,112},{24,120},{32,64},{40,72},{48,80},{56,88},{... | collective-permute-start | bytes 393224 | tf_op jit(solution)/shard_map/ppermute | solution.py:327
  54.8 1.3 %collective-permute-start.19 = (bf16[4,128,128]{2,1,0:T(8,128)(2,1)S(1)}, bf16[4,128,128]{2,1,0:T(8,128)(2,1)S(1)}, u32[]{:S(2)}, u32[]{:S(2)}) collective-permute-start(bf16[4,128,128]{2,1,0:T(8,128)(2,1)S(1)} %shard_map.95.refs_0_), channel_id=1, source_target_pairs={{0,80},{8,88},{16,64},{24,72},{32,112},{40,120},{48,96},{56,104},{... | collective-permute-start | bytes 393224 | tf_op jit(solution)/shard_map/ppermute | solution.py:327
  56.2 1.0 collective-permute-start.18
  57.2 2.4 %collective-permute-start.17 = (bf16[4,128,128]{2,1,0:T(8,128)(2,1)S(1)}, bf16[4,128,128]{2,1,0:T(8,128)(2,1)S(1)}, u32[]{:S(2)}, u32[]{:S(2)}) collective-permute-start(bf16[4,128,128]{2,1,0:T(8,128)(2,1)S(1)} %shard_map.95.refs_0_), channel_id=1, source_target_pairs={{0,48},{8,56},{16,32},{24,40},{32,16},{40,24},{48,0},{56,8},{64,11... | collective-permute-start | bytes 393224 | tf_op jit(solution)/shard_map/ppermute | solution.py:327
  59.6 1.2 %collective-permute-start.16 = (bf16[4,128,128]{2,1,0:T(8,128)(2,1)S(1)}, bf16[4,128,128]{2,1,0:T(8,128)(2,1)S(1)}, u32[]{:S(2)}, u32[]{:S(2)}) collective-permute-start(bf16[4,128,128]{2,1,0:T(8,128)(2,1)S(1)} %shard_map.95.refs_0_), channel_id=1, source_target_pairs={{0,32},{8,40},{16,48},{24,56},{32,0},{40,8},{48,16},{56,24},{64,96... | collective-permute-start | bytes 393224 | tf_op jit(solution)/shard_map/ppermute | solution.py:327
  60.8 2.0 %collective-permute-done.19.refs_5_ = bf16[4,128,128]{2,1,0:T(8,128)(2,1)S(1)} collective-permute-done((bf16[4,128,128]{2,1,0:T(8,128)(2,1)S(1)}, bf16[4,128,128]{2,1,0:T(8,128)(2,1)S(1)}, u32[]{:S(2)}, u32[]{:S(2)}) %collective-permute-start.19) | collective-permute-done | bytes 131104 | tf_op jit(solution)/shard_map/ppermute | solution.py:327
  62.8 2.3 %collective-permute-done.18.refs_4_ = bf16[4,128,128]{2,1,0:T(8,128)(2,1)S(1)} collective-permute-done((bf16[4,128,128]{2,1,0:T(8,128)(2,1)S(1)}, bf16[4,128,128]{2,1,0:T(8,128)(2,1)S(1)}, u32[]{:S(2)}, u32[]{:S(2)}) %collective-permute-start.18) | collective-permute-done | bytes 131104 | tf_op jit(solution)/shard_map/ppermute | solution.py:327
  65.0 1.4 %collective-permute-done.16.refs_2_ = bf16[4,128,128]{2,1,0:T(8,128)(2,1)S(1)} collective-permute-done((bf16[4,128,128]{2,1,0:T(8,128)(2,1)S(1)}, bf16[4,128,128]{2,1,0:T(8,128)(2,1)S(1)}, u32[]{:S(2)}, u32[]{:S(2)}) %collective-permute-start.16) | collective-permute-done | bytes 131104 | tf_op jit(solution)/shard_map/ppermute | solution.py:327
  66.5 1.9 %collective-permute-done.15.refs_1_ = bf16[4,128,128]{2,1,0:T(8,128)(2,1)S(1)} collective-permute-done((bf16[4,128,128]{2,1,0:T(8,128)(2,1)S(1)}, bf16[4,128,128]{2,1,0:T(8,128)(2,1)S(1)}, u32[]{:S(2)}, u32[]{:S(2)}) %collective-permute-start.15) | collective-permute-done | bytes 131104 | tf_op jit(solution)/shard_map/ppermute | solution.py:327
  68.3 0.1 shard_map.96.mean_ref
  68.4 1.8 %collective-permute-start.22 = (bf16[32,128,128]{2,1,0:T(8,128)(2,1)S(1)}, bf16[32,128,128]{2,1,0:T(8,128)(2,1)S(1)}, u32[]{:S(2)}, u32[]{:S(2)}) collective-permute-start(bf16[32,128,128]{2,1,0:T(8,128)(2,1)S(1)} %shard_map.96.mean_ref), channel_id=1, source_target_pairs={{0,8},{8,0},{16,24},{24,16},{32,40},{40,32},{48,56},{56,48},{64,72... | collective-permute-start | bytes 3145736 | tf_op jit(solution)/shard_map/ppermute | solution.py:388
  70.3 4.0 %shard_map.97.refs_0_ = f32[32,272,128]{2,1,0:T(8,128)S(1)} custom-call(s32[8,128]{1,0:T(8,128)S(1)} %get-tuple-element.20.list_ref, bf16[32,128,128]{2,1,0:T(8,128)(2,1)S(1)} %shard_map.96.mean_ref, bf16[256,128]{1,0:T(8,128)(2,1)S(1)} %get-tuple-element.33.weight_ref, f32[256,128]{1,0:T(8,128)S(1)} %get-tuple-element.34.bias_ref, ...), custom_call_target="tpu_custom_call" | custom-call | flops 6000000000 | bytes 18000000 | tf_op jit(solution)/shard_map/pallas_call | solution.py:392
  74.3 0.0 collective-permute-done.22.mean_ref
  74.3 4.8 %shard_map.98 = bf16[8,1040,128]{2,1,0:T(8,128)(2,1)S(1)} custom-call(s32[8,128]{1,0:T(8,128)S(1)} %get-tuple-element.20.list_ref, bf16[32,128,128]{2,1,0:T(8,128)(2,1)S(1)} %collective-permute-done.22.mean_ref, bf16[256,128]{1,0:T(8,128)(2,1)S(1)} %get-tuple-element.33.weight_ref, f32[256,128]{1,0:T(8,128)S(1)} %get-tuple-element.34.bias_ref, ...), custom_call_target="tpu_custom_call" | custom-call | flops 6000000000 | bytes 18000000 | tf_op jit(solution)/shard_map/pallas_call | solution.py:400
  79.1 0.0 copy-start.1
  79.1 0.0 copy-start.2
  79.2 37.5 %all_to_all.5.parts_ref = bf16[8,1040,128]{2,1,0:T(8,128)(2,1)S(1)} all-to-all(bf16[8,1040,128]{2,1,0:T(8,128)(2,1)S(1)} %shard_map.98), channel_id=1, replica_groups=mesh['row'=16,'col'=8] {'col'}, dimensions={0} | all-to-all | bytes 4259840 | tf_op jit(solution)/shard_map/all_to_all | solution.py:408
  116.7 1.2 %shard_map.99 = bf16[512,256]{1,0:T(8,128)(2,1)} custom-call(bf16[256,256]{1,0:T(8,128)(2,1)S(1)} %copy-done.1, f32[1,256]{1,0:T(1,128)S(1)} %bitcast.5, bf16[8,1040,128]{2,1,0:T(8,128)(2,1)S(1)} %all_to_all.5.parts_ref), custom_call_target="tpu_custom_call" | custom-call | flops 1000000000 | bytes 3000000 | tf_op jit(solution)/shard_map/pallas_call | solution.py:409
  (14 shorter events, 0.0 us)
Async XLA Ops:
  0.0 9.7 %collective-permute-start.5 = (bf16[512,128]{1,0:T(8,128)(2,1)}, bf16[512,128]{1,0:T(8,128)(2,1)S(1)}, u32[]{:S(2)}, u32[]{:S(2)}) collective-permute-start(bf16[512,128]{1,0:T(8,128)(2,1)} %refs_0_.1), channel_id=1, source_target_pairs={{0,6},{1,7},{2,4},{3,5},{4,2},{5,3},{6,0},{7,1},{8,14},{9,15},{10,... | collective-permute-start | bytes 393224 | tf_op jit(solution)/shard_map/ppermute | solution.py:327
  4.6 6.4 %collective-permute-start.4 = (bf16[512,128]{1,0:T(8,128)(2,1)}, bf16[512,128]{1,0:T(8,128)(2,1)S(1)}, u32[]{:S(2)}, u32[]{:S(2)}) collective-permute-start(bf16[512,128]{1,0:T(8,128)(2,1)} %refs_0_.1), channel_id=1, source_target_pairs={{0,5},{1,4},{2,7},{3,6},{4,1},{5,0},{6,3},{7,2},{8,13},{9,12},{10,... | collective-permute-start | bytes 393224 | tf_op jit(solution)/shard_map/ppermute | solution.py:327
  4.8 12.3 %collective-permute-start.3 = (bf16[512,128]{1,0:T(8,128)(2,1)}, bf16[512,128]{1,0:T(8,128)(2,1)S(1)}, u32[]{:S(2)}, u32[]{:S(2)}) collective-permute-start(bf16[512,128]{1,0:T(8,128)(2,1)} %refs_0_.1), channel_id=1, source_target_pairs={{0,4},{1,5},{2,6},{3,7},{4,0},{5,1},{6,2},{7,3},{8,12},{9,13},{10,... | collective-permute-start | bytes 393224 | tf_op jit(solution)/shard_map/ppermute | solution.py:327
  6.1 11.0 %collective-permute-start.2 = (bf16[512,128]{1,0:T(8,128)(2,1)}, bf16[512,128]{1,0:T(8,128)(2,1)S(1)}, u32[]{:S(2)}, u32[]{:S(2)}) collective-permute-start(bf16[512,128]{1,0:T(8,128)(2,1)} %refs_0_.1), channel_id=1, source_target_pairs={{0,3},{1,2},{2,1},{3,0},{4,7},{5,6},{6,5},{7,4},{8,11},{9,10},{10,... | collective-permute-start | bytes 393224 | tf_op jit(solution)/shard_map/ppermute | solution.py:327
  6.3 10.8 %collective-permute-start.1 = (bf16[512,128]{1,0:T(8,128)(2,1)}, bf16[512,128]{1,0:T(8,128)(2,1)S(1)}, u32[]{:S(2)}, u32[]{:S(2)}) collective-permute-start(bf16[512,128]{1,0:T(8,128)(2,1)} %refs_0_.1), channel_id=1, source_target_pairs={{0,2},{1,3},{2,0},{3,1},{4,6},{5,7},{6,4},{7,5},{8,10},{9,11},{10,... | collective-permute-start | bytes 393224 | tf_op jit(solution)/shard_map/ppermute | solution.py:327
  9.7 7.4 %collective-permute-start = (bf16[512,128]{1,0:T(8,128)(2,1)}, bf16[512,128]{1,0:T(8,128)(2,1)S(1)}, u32[]{:S(2)}, u32[]{:S(2)}) collective-permute-start(bf16[512,128]{1,0:T(8,128)(2,1)} %refs_0_.1), channel_id=1, source_target_pairs={{0,1},{1,0},{2,3},{3,2},{4,5},{5,4},{6,7},{7,6},{8,9},{9,8},{10,11... | collective-permute-start | bytes 393224 | tf_op jit(solution)/shard_map/ppermute | solution.py:327
  11.0 6.4 %collective-permute-start.6 = (bf16[512,128]{1,0:T(8,128)(2,1)}, bf16[512,128]{1,0:T(8,128)(2,1)S(1)}, u32[]{:S(2)}, u32[]{:S(2)}) collective-permute-start(bf16[512,128]{1,0:T(8,128)(2,1)} %refs_0_.1), channel_id=1, source_target_pairs={{0,7},{1,6},{2,5},{3,4},{4,3},{5,2},{6,1},{7,0},{8,15},{9,14},{10,... | collective-permute-start | bytes 393224 | tf_op jit(solution)/shard_map/ppermute | solution.py:327
  13.0 4.4 %copy-start = (bf16[512,128]{1,0:T(8,128)(2,1)S(1)}, bf16[512,128]{1,0:T(8,128)(2,1)}, u32[]{:S(2)}) copy-start(bf16[512,128]{1,0:T(8,128)(2,1)} %refs_0_.1) | copy-start | bytes 393220
  20.6 5.7 %collective-permute-start.7 = (bf16[8,528,128]{2,1,0:T(8,128)(2,1)S(1)}, bf16[8,528,128]{2,1,0:T(8,128)(2,1)S(1)}, u32[]{:S(2)}, u32[]{:S(2)}) collective-permute-start(bf16[8,528,128]{2,1,0:T(8,128)(2,1)S(1)} %get-tuple-element.24), channel_id=1, source_target_pairs={{0,8},{8,0},{16,24},{24,16},{32,40},{40,32},{48,56},{56,48},{64,72... | collective-permute-start | bytes 3244040 | tf_op jit(solution)/shard_map/ppermute | solution.py:373
  26.5 12.6 %collective-permute-start.8 = (bf16[528,128]{1,0:T(8,128)(2,1)S(1)}, bf16[528,128]{1,0:T(8,128)(2,1)S(1)}, u32[]{:S(2)}, u32[]{:S(2)}) collective-permute-start(bf16[528,128]{1,0:T(8,128)(2,1)S(1)} %get-tuple-element.25), channel_id=1, source_target_pairs={{0,112},{8,120},{16,96},{24,104},{32,80},{40,88},{48,64},{56,72},{... | collective-permute-start | bytes 405512 | tf_op jit(solution)/shard_map/ppermute | solution.py:327
  33.4 7.9 %collective-permute-start.9 = (bf16[528,128]{1,0:T(8,128)(2,1)S(1)}, bf16[528,128]{1,0:T(8,128)(2,1)S(1)}, u32[]{:S(2)}, u32[]{:S(2)}) collective-permute-start(bf16[528,128]{1,0:T(8,128)(2,1)S(1)} %get-tuple-element.26), channel_id=1, source_target_pairs={{0,96},{8,104},{16,112},{24,120},{32,64},{40,72},{48,80},{56,88},{... | collective-permute-start | bytes 405512 | tf_op jit(solution)/shard_map/ppermute | solution.py:327
  33.4 9.5 %collective-permute-start.10 = (bf16[528,128]{1,0:T(8,128)(2,1)S(1)}, bf16[528,128]{1,0:T(8,128)(2,1)S(1)}, u32[]{:S(2)}, u32[]{:S(2)}) collective-permute-start(bf16[528,128]{1,0:T(8,128)(2,1)S(1)} %get-tuple-element.27), channel_id=1, source_target_pairs={{0,80},{8,88},{16,64},{24,72},{32,112},{40,120},{48,96},{56,104},{... | collective-permute-start | bytes 405512 | tf_op jit(solution)/shard_map/ppermute | solution.py:327
  34.5 11.3 %collective-permute-start.11 = (bf16[528,128]{1,0:T(8,128)(2,1)S(1)}, bf16[528,128]{1,0:T(8,128)(2,1)S(1)}, u32[]{:S(2)}, u32[]{:S(2)}) collective-permute-start(bf16[528,128]{1,0:T(8,128)(2,1)S(1)} %get-tuple-element.28), channel_id=1, source_target_pairs={{0,64},{8,72},{16,80},{24,88},{32,96},{40,104},{48,112},{56,120},{... | collective-permute-start | bytes 405512 | tf_op jit(solution)/shard_map/ppermute | solution.py:327
  36.8 9.0 %collective-permute-start.12 = (bf16[528,128]{1,0:T(8,128)(2,1)S(1)}, bf16[528,128]{1,0:T(8,128)(2,1)S(1)}, u32[]{:S(2)}, u32[]{:S(2)}) collective-permute-start(bf16[528,128]{1,0:T(8,128)(2,1)S(1)} %get-tuple-element.29), channel_id=1, source_target_pairs={{0,48},{8,56},{16,32},{24,40},{32,16},{40,24},{48,0},{56,8},{64,11... | collective-permute-start | bytes 405512 | tf_op jit(solution)/shard_map/ppermute | solution.py:327
  39.1 8.7 %collective-permute-start.13 = (bf16[528,128]{1,0:T(8,128)(2,1)S(1)}, bf16[528,128]{1,0:T(8,128)(2,1)S(1)}, u32[]{:S(2)}, u32[]{:S(2)}) collective-permute-start(bf16[528,128]{1,0:T(8,128)(2,1)S(1)} %get-tuple-element.30), channel_id=1, source_target_pairs={{0,32},{8,40},{16,48},{24,56},{32,0},{40,8},{48,16},{56,24},{64,96... | collective-permute-start | bytes 405512 | tf_op jit(solution)/shard_map/ppermute | solution.py:327
  41.3 6.9 %collective-permute-start.14 = (bf16[528,128]{1,0:T(8,128)(2,1)S(1)}, bf16[528,128]{1,0:T(8,128)(2,1)S(1)}, u32[]{:S(2)}, u32[]{:S(2)}) collective-permute-start(bf16[528,128]{1,0:T(8,128)(2,1)S(1)} %get-tuple-element.31), channel_id=1, source_target_pairs={{0,16},{8,24},{16,0},{24,8},{32,48},{40,56},{48,32},{56,40},{64,80... | collective-permute-start | bytes 405512 | tf_op jit(solution)/shard_map/ppermute | solution.py:327
  48.4 11.2 %collective-permute-start.21 = (bf16[4,128,128]{2,1,0:T(8,128)(2,1)S(1)}, bf16[4,128,128]{2,1,0:T(8,128)(2,1)S(1)}, u32[]{:S(2)}, u32[]{:S(2)}) collective-permute-start(bf16[4,128,128]{2,1,0:T(8,128)(2,1)S(1)} %shard_map.95.refs_0_), channel_id=1, source_target_pairs={{0,112},{8,120},{16,96},{24,104},{32,80},{40,88},{48,64},{56,72},{... | collective-permute-start | bytes 393224 | tf_op jit(solution)/shard_map/ppermute | solution.py:327
  50.7 10.1 %collective-permute-start.20 = (bf16[4,128,128]{2,1,0:T(8,128)(2,1)S(1)}, bf16[4,128,128]{2,1,0:T(8,128)(2,1)S(1)}, u32[]{:S(2)}, u32[]{:S(2)}) collective-permute-start(bf16[4,128,128]{2,1,0:T(8,128)(2,1)S(1)} %shard_map.95.refs_0_), channel_id=1, source_target_pairs={{0,96},{8,104},{16,112},{24,120},{32,64},{40,72},{48,80},{56,88},{... | collective-permute-start | bytes 393224 | tf_op jit(solution)/shard_map/ppermute | solution.py:327
  54.8 7.9 %collective-permute-start.19 = (bf16[4,128,128]{2,1,0:T(8,128)(2,1)S(1)}, bf16[4,128,128]{2,1,0:T(8,128)(2,1)S(1)}, u32[]{:S(2)}, u32[]{:S(2)}) collective-permute-start(bf16[4,128,128]{2,1,0:T(8,128)(2,1)S(1)} %shard_map.95.refs_0_), channel_id=1, source_target_pairs={{0,80},{8,88},{16,64},{24,72},{32,112},{40,120},{48,96},{56,104},{... | collective-permute-start | bytes 393224 | tf_op jit(solution)/shard_map/ppermute | solution.py:327
  56.2 8.9 %collective-permute-start.18 = (bf16[4,128,128]{2,1,0:T(8,128)(2,1)S(1)}, bf16[4,128,128]{2,1,0:T(8,128)(2,1)S(1)}, u32[]{:S(2)}, u32[]{:S(2)}) collective-permute-start(bf16[4,128,128]{2,1,0:T(8,128)(2,1)S(1)} %shard_map.95.refs_0_), channel_id=1, source_target_pairs={{0,64},{8,72},{16,80},{24,88},{32,96},{40,104},{48,112},{56,120},{... | collective-permute-start | bytes 393224 | tf_op jit(solution)/shard_map/ppermute | solution.py:327
  57.2 7.8 %collective-permute-start.17 = (bf16[4,128,128]{2,1,0:T(8,128)(2,1)S(1)}, bf16[4,128,128]{2,1,0:T(8,128)(2,1)S(1)}, u32[]{:S(2)}, u32[]{:S(2)}) collective-permute-start(bf16[4,128,128]{2,1,0:T(8,128)(2,1)S(1)} %shard_map.95.refs_0_), channel_id=1, source_target_pairs={{0,48},{8,56},{16,32},{24,40},{32,16},{40,24},{48,0},{56,8},{64,11... | collective-permute-start | bytes 393224 | tf_op jit(solution)/shard_map/ppermute | solution.py:327
  59.6 6.9 %collective-permute-start.16 = (bf16[4,128,128]{2,1,0:T(8,128)(2,1)S(1)}, bf16[4,128,128]{2,1,0:T(8,128)(2,1)S(1)}, u32[]{:S(2)}, u32[]{:S(2)}) collective-permute-start(bf16[4,128,128]{2,1,0:T(8,128)(2,1)S(1)} %shard_map.95.refs_0_), channel_id=1, source_target_pairs={{0,32},{8,40},{16,48},{24,56},{32,0},{40,8},{48,16},{56,24},{64,96... | collective-permute-start | bytes 393224 | tf_op jit(solution)/shard_map/ppermute | solution.py:327
  60.8 7.5 %collective-permute-start.15 = (bf16[4,128,128]{2,1,0:T(8,128)(2,1)S(1)}, bf16[4,128,128]{2,1,0:T(8,128)(2,1)S(1)}, u32[]{:S(2)}, u32[]{:S(2)}) collective-permute-start(bf16[4,128,128]{2,1,0:T(8,128)(2,1)S(1)} %shard_map.95.refs_0_), channel_id=1, source_target_pairs={{0,16},{8,24},{16,0},{24,8},{32,48},{40,56},{48,32},{56,40},{64,80... | collective-permute-start | bytes 393224 | tf_op jit(solution)/shard_map/ppermute | solution.py:327
  68.4 5.9 %collective-permute-start.22 = (bf16[32,128,128]{2,1,0:T(8,128)(2,1)S(1)}, bf16[32,128,128]{2,1,0:T(8,128)(2,1)S(1)}, u32[]{:S(2)}, u32[]{:S(2)}) collective-permute-start(bf16[32,128,128]{2,1,0:T(8,128)(2,1)S(1)} %shard_map.96.mean_ref), channel_id=1, source_target_pairs={{0,8},{8,0},{16,24},{24,16},{32,40},{40,32},{48,56},{56,48},{64,72... | collective-permute-start | bytes 3145736 | tf_op jit(solution)/shard_map/ppermute | solution.py:388
  79.1 37.5 %copy-start.1 = (bf16[256,256]{1,0:T(8,128)(2,1)S(1)}, bf16[256,256]{1,0:T(8,128)(2,1)}, u32[]{:S(2)}) copy-start(bf16[256,256]{1,0:T(8,128)(2,1)} %weight_ref.3) | copy-start | bytes 393220
  79.1 37.5 %copy-start.2 = (f32[256]{0:T(256)S(1)}, f32[256]{0:T(256)}, u32[]{:S(2)}) copy-start(f32[256]{0:T(256)} %param.17) | copy-start | bytes 3076
